TPU v7x, 768 devices: a whole 4x8x12 slice. The times are simulated.
768 devices in a mesh: grp: 32 (over z_lo, y), shard: 24 (over z_hi, x, core).
Axes of the slice: x: 4, y: 8, z: 12 (z_hi: 3, z_lo: 4; z = z_hi * 4 + z_lo), core: 2. Of those that a mesh axis runs over, the one named last changes fastest.
Arguments:
- features: bfloat16 [196608, 1536], P(('grp', 'shard')), may hold values from -6 to 6
- w_in: bfloat16 [1536, 1024], replicated, may hold values from -0.15625 to 0.15625
- upstream: bfloat16 [196608, 1024], P(('grp', 'shard')), may hold values from -6 to 6
- hot_ids: int32 [196608, 8], P(('grp', 'shard')), may hold values from 0 to 6143
- cold_rows: int32 [786432], P(('grp', 'shard')), may hold values from 0 to 2047
- cold_owner: int32 [786432, 1], P(('grp', 'shard')), may hold values from 0 to 23; in each aligned block of 1024 rows (0 to 1023, 1024 to 2047, ...) at most 170 rows name the same one
- hot_table: float32 [6144, 128], P('shard'), may hold values from -6 to 6
- hot_accum: float32 [6144], P('shard'), may hold values from 1 to 1000
- cold_table: float32 [1572864, 128], P(('grp', 'shard')), may hold values from -6 to 6
- cold_accum: float32 [1572864], P(('grp', 'shard')), may hold values from 1 to 1000
Outputs:
- hot_new: float32 [6144, 128], P('shard')
- hot_accum_new: float32 [6144], P('shard')
- cold_new: float32 [1572864, 128], P(('grp', 'shard'))
- cold_accum_new: float32 [1572864], P(('grp', 'shard'))
Inputs may be any that keep to these rules, and one draw needn't show every extreme that they name: `cold_owner`: among the 1024 lookups of one device, no owner is named more than 170 times, a bound that some block reaches.
All inputs are finite; a program needn't handle non-finite values.
Results may differ from a plain program's by a relative error of at most 0.0024.
Values may be sent and summed in bfloat16 or wider, within the bound.
A program may use at most 64 MiB of HBM per device.

v0:
```python
import jax
import jax.numpy as jnp
from jax import lax
from jax.sharding import PartitionSpec as P

learn_rate = 0.5


def adagrad(rows, accum, grads):
    accum_new = accum + jnp.mean(grads * grads, axis=1)
    return (rows - learn_rate * grads / jnp.sqrt(accum_new)[:, None], accum_new)


def shards(
    features,
    w_in,
    upstream,
    hot_ids,
    cold_rows,
    cold_owner,
    hot_table,
    hot_accum,
    cold_table,
    cold_accum,
):
    width = hot_table.shape[1]
    hot_width = hot_ids.shape[1] * width
    preact = jnp.dot(features, w_in, preferred_element_type=jnp.float32)
    sigm = jax.nn.sigmoid(preact)
    delta = (upstream.astype(jnp.float32) * sigm * (1.0 + preact * (1.0 - sigm))).astype(
        jnp.bfloat16
    )
    cold_grad = (
        jnp.dot(delta, w_in[hot_width:].T, preferred_element_type=jnp.float32)
        .astype(jnp.bfloat16)
        .reshape(-1, width)
    )
    owners = cold_owner[:, 0]
    peers = lax.axis_size("shard")
    capacity = 4 * owners.shape[0] // peers
    one_hot = (owners[:, None] == jnp.arange(peers, dtype=jnp.int32)[None, :]).astype(jnp.int32)
    places = jnp.sum((jnp.cumsum(one_hot, axis=0) - 1) * one_hot, axis=1)
    outgoing = jnp.zeros((peers, capacity, width), jnp.bfloat16).at[owners, places].set(cold_grad)
    outgoing_ids = jnp.zeros((peers, capacity), jnp.int32).at[owners, places].set(cold_rows)
    arrived, arrived_ids = (
        lax.all_to_all(outgoing, "shard", split_axis=0, concat_axis=0, tiled=True),
        lax.all_to_all(outgoing_ids, "shard", split_axis=0, concat_axis=0, tiled=True),
    )
    cold_sum = jax.ops.segment_sum(
        arrived.reshape(-1, width).astype(jnp.float32),
        arrived_ids.reshape(-1),
        num_segments=cold_table.shape[0],
    )
    cold_new, cold_accum_new = adagrad(cold_table, cold_accum, cold_sum)
    hot_grad = (
        jnp.dot(delta, w_in[:hot_width].T, preferred_element_type=jnp.float32)
        .astype(jnp.bfloat16)
        .reshape(-1, width)
    )
    owned = hot_table.shape[0]
    partial_value = jax.ops.segment_sum(
        hot_grad.astype(jnp.float32), hot_ids.reshape(-1), num_segments=owned * peers
    )
    mine = lax.psum_scatter(partial_value, "shard", scatter_dimension=0, tiled=True)
    total = lax.psum(mine, "grp")
    hot_new, hot_accum_new = adagrad(hot_table, hot_accum, total)
    return (hot_new, hot_accum_new, cold_new, cold_accum_new)


def solution(mesh):
    placed = (
        P(("grp", "shard"), None),
        P(),
        P(("grp", "shard"), None),
        P(("grp", "shard"), None),
        P(("grp", "shard")),
        P(("grp", "shard"), None),
        P("shard", None),
        P("shard"),
        P(("grp", "shard"), None),
        P(("grp", "shard")),
    )
    return jax.shard_map(
        shards,
        mesh=mesh,
        in_specs=placed,
        out_specs=(P("shard", None), P("shard"), P(("grp", "shard"), None), P(("grp", "shard"))),
        check_vma=False,
    )
```

profile of v0, /device:TPU:2, one launch (start us, length us, event | category | flops | bytes accessed | tf_op | source)
XLA Modules:
  0.0 486.7 jit_solution(9673374448269935368)
XLA Ops:
  7.2 0.0 copy-start
  7.2 0.0 reduce-scatter.2.cloned.1.call-start
  7.2 0.9 copy.18
  8.1 0.1 reshape.68
  8.2 0.1 copy-done
  8.3 0.0 copy-start.9
  8.3 3.4 multiply_convert_fusion
  11.7 0.0 copy-done.9
  11.7 0.7 fusion.7
  12.5 0.2 reshape.70
  12.7 0.0 copy-start.3
  12.7 0.0 copy-start.8
  12.7 0.0 copy-start.6
  12.7 0.0 copy-start.7
  12.7 13.3 %scatter_custom_fusion = f32[6144,128]{1,0:T(8,128)} fusion(s32[2048]{0:T(1024)S(1)} %reshape.68, f32[2048,128]{1,0:T(8,128)S(1)} %reshape.70, f32[]{:T(128)} %constant.9.clone.1), kind=kCustom, calls=%fused_computation.6 | custom fusion | flops 262144 | bytes 3145732 | tf_op jit(solution)/shard_map/scatter-add | solution.py:61
  26.0 0.0 reduce-scatter.2.cloned.1.call-update
  26.0 0.0 copy-done.3
  26.0 6.8 %reduce-window.6 = s32[24,8,128]{2,1,0:T(8,128)S(1)} reduce-window(s32[24,8,128]{2,1,0:T(8,128)S(1)} %fusion.17, s32[]{:T(128)} %constant.13.clone.1), window={size=1x1x128 pad=0_0x0_0x127_0}, to_apply=%region_4.5 | reduce-window | flops 3121152 | bytes 196612 | tf_op jit(solution)/shard_map/reduce-window
  32.8 0.1 slice.16
  32.9 0.1 copy.19
  33.0 0.1 copy.20
  33.1 0.1 add_add_fusion
  33.3 0.0 copy-done.8
  33.3 0.1 and_reduce_fusion
  33.4 0.0 copy-done.6
  33.4 0.0 copy-done.7
  33.4 0.1 multiply_reduce_fusion.2
  33.5 4.5 scatter_custom_fusion.2
  38.0 0.7 all_to_all.9
  38.8 17.0 %all-to-all-start = ((s32[24,1,170]{2,1,0:T(1,128)}), s32[24,1,170]{2,1,0:T(1,128)S(1)}, u32[]{:S(2)}, u32[]{:S(2)}) async-start(s32[24,1,170]{2,1,0:T(1,128)} %all_to_all.9), calls=%async_computation.1 | async-start | bytes 49152 | tf_op jit(solution)/shard_map/all_to_all | solution.py:47
  55.8 1.7 convolution_convert_fusion
  57.5 0.2 reshape.90
  57.7 3.5 scatter_custom_fusion.3
  61.2 1.1 copy.21
  62.4 2.1 all-to-all-done
  64.4 7.6 %all-to-all-start.1 = ((bf16[24,170,128]{2,1,0:T(8,128)(2,1)}), bf16[24,170,128]{2,1,0:T(8,128)(2,1)S(1)}, u32[]{:S(2)}, u32[]{:S(2)}) async-start(bf16[24,170,128]{2,1,0:T(8,128)(2,1)} %copy.21), calls=%async_computation.2 | async-start | bytes 2162688 | tf_op jit(solution)/shard_map/all_to_all | solution.py:46
  72.1 0.0 copy-start.4
  72.1 0.0 copy-start.1
  72.1 0.2 all-reduce.2.cloned.1.call-start
  72.3 0.1 reduce.4
  72.4 0.1 reshape.76
  72.5 46.2 %all-to-all-done.1 = bf16[24,170,128]{2,1,0:T(8,128)(2,1)S(1)} async-done(((bf16[24,170,128]{2,1,0:T(8,128)(2,1)}), bf16[24,170,128]{2,1,0:T(8,128)(2,1)S(1)}, u32[]{:S(2)}, u32[]{:S(2)}) %all-to-all-start.1) | async-done | bytes 1044512 | tf_op jit(solution)/shard_map/all_to_all | solution.py:46
  118.7 1.5 reshape.78
  120.2 0.0 copy-start.5
  120.2 0.0 copy-start.2
  120.2 28.1 %scatter_custom_fusion.1 = f32[2048,128]{1,0:T(8,128)S(1)} fusion(s32[4080]{0:T(1024)S(1)} %reshape.76, f32[4080,128]{1,0:T(8,128)} %reshape.78, f32[]{:T(128)} %constant.9.clone.1), kind=kCustom, calls=%fused_computation.15 | custom fusion | flops 522240 | bytes 1049088 | tf_op jit(solution)/shard_map/scatter-add | solution.py:49
  148.3 0.3 multiply_reduce_fusion
  148.7 0.0 copy-done.4
  148.7 0.6 fusion.20
  149.3 43.4 %reduce-scatter.2.cloned.1.call-done = f32[256,128]{1,0:T(8,128)} async-done(((f32[6144,128]{1,0:T(8,128)}), f32[256,128]{1,0:T(8,128)}) %reduce-scatter.2.cloned.1.call-update) | async-done | bytes 131088 | tf_op jit(solution)/shard_map/reduce_scatter | solution.py:64
  192.7 0.0 all-reduce.2.cloned.1.call-update
  192.8 0.0 copy-done.1
  192.8 1.3 divide_subtract_fusion
  194.1 282.6 %all-reduce.2.cloned.1.call-done = f32[256,128]{1,0:T(8,128)} async-done(((f32[256,128]{1,0:T(8,128)}), f32[256,128]{1,0:T(8,128)}) %all-reduce.2.cloned.1.call-update) | async-done | bytes 131088 | tf_op jit(solution)/shard_map/psum | solution.py:65
  476.6 1.0 multiply_reduce_fusion.1
  477.7 0.0 copy-done.5
  477.7 0.6 fusion.21
  478.2 0.0 copy-done.2
  478.2 1.7 divide_subtract_fusion.1
  (6 shorter events, 0.1 us)
Async XLA Ops:
  7.2 1.2 copy-start
  7.2 185.5 %reduce-scatter.2.cloned.1.call-start = ((), (), s32[]{:S(2)}) async-start(), calls=%async_computation.3 | async-start | bytes 3276800 | tf_op jit(solution)/shard_map/reduce_scatter | solution.py:64
  8.3 3.4 copy-start.9
  12.7 13.3 %copy-start.3 = (s32[1024,1]{0,1:T(1,128)S(1)}, s32[1024,1]{0,1:T(1,128)}, u32[]{:S(2)}) copy-start(s32[1024,1]{0,1:T(1,128)} %param.15) | copy-start | bytes 12292
  12.7 20.6 %copy-start.8 = (s32[2]{0:T(128)S(1)}, s32[2]{0:T(128)}, u32[]{:S(2)}) copy-start(s32[2]{0:T(128)} %constant.43) | copy-start | bytes 28
  12.7 20.7 %copy-start.6 = (s32[2]{0:T(128)S(1)}, s32[2]{0:T(128)}, u32[]{:S(2)}) copy-start(s32[2]{0:T(128)} %constant.46) | copy-start | bytes 28
  12.7 20.7 %copy-start.7 = (s32[2]{0:T(128)S(1)}, s32[2]{0:T(128)}, u32[]{:S(2)}) copy-start(s32[2]{0:T(128)} %constant.40) | copy-start | bytes 28
  38.8 25.7 %all-to-all-start = ((s32[24,1,170]{2,1,0:T(1,128)}), s32[24,1,170]{2,1,0:T(1,128)S(1)}, u32[]{:S(2)}, u32[]{:S(2)}) async-start(s32[24,1,170]{2,1,0:T(1,128)} %all_to_all.9), calls=%async_computation.1 | async-start | bytes 49152 | tf_op jit(solution)/shard_map/all_to_all | solution.py:47
  64.4 54.3 %all-to-all-start.1 = ((bf16[24,170,128]{2,1,0:T(8,128)(2,1)}), bf16[24,170,128]{2,1,0:T(8,128)(2,1)S(1)}, u32[]{:S(2)}, u32[]{:S(2)}) async-start(bf16[24,170,128]{2,1,0:T(8,128)(2,1)} %copy.21), calls=%async_computation.2 | async-start | bytes 2162688 | tf_op jit(solution)/shard_map/all_to_all | solution.py:46
  72.1 76.6 %copy-start.4 = (f32[2048]{0:T(1024)S(1)}, f32[2048]{0:T(1024)}, u32[]{:S(2)}) copy-start(f32[2048]{0:T(1024)} %param.19) | copy-start | bytes 24580
  72.1 120.7 %copy-start.1 = (f32[2048,128]{1,0:T(8,128)S(1)}, f32[2048,128]{1,0:T(8,128)}, u32[]{:S(2)}) copy-start(f32[2048,128]{1,0:T(8,128)} %param.18) | copy-start | bytes 3145732
  72.1 404.5 %all-reduce.2.cloned.1.call-start = ((), (), s32[]{:S(2)}) async-start(), calls=%async_computation.4 | async-start | bytes 262144 | tf_op jit(solution)/shard_map/psum | solution.py:65
  120.2 357.5 %copy-start.5 = (f32[256]{0:T(256)S(1)}, f32[256]{0:T(256)}, u32[]{:S(2)}) copy-start(f32[256]{0:T(256)} %param.17) | copy-start | bytes 3076
  120.2 358.1 %copy-start.2 = (f32[256,128]{1,0:T(8,128)S(1)}, f32[256,128]{1,0:T(8,128)}, u32[]{:S(2)}) copy-start(f32[256,128]{1,0:T(8,128)} %param.16) | copy-start | bytes 393220
Sparse Core Ops, SparseCore 0:
  26.1 166.5 reduce-scatter.1
  195.9 280.6 all-reduce.1
where the time goes:
time: 487 us
  waiting for transfers between devices  374 us (77%)
  other arithmetic  54.1 us (11%)
  starting transfers between devices  24.9 us (5%)
  between operations  14.3 us (3%)
  local copies, waits for them, and re-layouts  13.3 us (3%)
  matrix products  5.88 us (1%)
    psum x1, waiting for transfers between devices, shards(): total = lax.psum(mine, 'grp')  283 us
    all_to_all x1, waiting for transfers between devices, shards(): lax.all_to_all(outgoing, 'shard', split_axis=0, concat_axis=0, tiled=True)  46.2 us
    reduce_scatter x1, waiting for transfers between devices, shards(): lax.psum_scatter(partial_value, 'shard', scatter_dimension=0, tiled=True)  43.4 us
    scatter-add x1, other arithmetic, shards(): jax.ops.segment_sum(arrived.reshape(-1, width).astype(jnp.float32), arriv...  28.1 us
    all_to_all x1, starting transfers between devices, shards(): lax.all_to_all(outgoing_ids, 'shard', split_axis=0, concat_axis=0, tiled=...  17 us
    scatter-add x1, other arithmetic, shards(): jax.ops.segment_sum(hot_grad.astype(jnp.float32), hot_ids.reshape(-1), nu...  13.3 us
  transfers between devices with their start and end apart: 4, of which 4 were waited for; matrix products, arithmetic and copies ran while one was open for 10% of the time, Pallas kernels for 0%

commit v1 on v0

v1 whole, which is shorter than its diff:
```python
import jax
import jax.numpy as jnp
from jax import lax
from jax.experimental import pallas as pl
from jax.experimental.pallas import tpu as pltpu
from jax.sharding import PartitionSpec as P

MESH = pl.DeviceIdType.MESH
learn_rate = 0.5

E = 128
SAMPLES = 256
HOT_FIELDS, COLD_FIELDS = 8, 4
OWNERS = 24
SLOTS = 176
USED = 170
HEAD = 168
DEPTH = 256
OWNED = 2048
STEP = 256
BF16, F32, I32 = jnp.bfloat16, jnp.float32, jnp.int32


def iota(shape, axis):
    return lax.broadcasted_iota(I32, shape, axis)


def nt_dot(a, b):
    return lax.dot_general(a, b, (((1,), (1,)), ((), ())), preferred_element_type=F32)


def dot(a, b):
    return jnp.dot(a, b, preferred_element_type=F32)


def grads_kernel(
    feat_ref, w_ref, up_ref, hid_ref, row_ref, own_ref, hotg_ref, gext_ref, key_ref, hidt_ref, acc, cold
):
    step = pl.program_id(0)
    w = w_ref[...]
    preact = dot(feat_ref[...], w)
    sigm = jax.nn.sigmoid(preact)
    delta = (up_ref[...].astype(F32) * sigm * (1.0 + preact * (1.0 - sigm))).astype(BF16)
    part = nt_dot(delta, w)

    @pl.when(step == 0)
    def _():
        acc[...] = part
        hidt_ref[...] = hid_ref[...].T
        owner = own_ref[...]
        named = (owner == iota((32, 4 * SAMPLES), 0)).astype(F32)
        before = (iota((256, 256), 0) < iota((256, 256), 1)).astype(BF16)
        carry = jnp.zeros((32, 1), F32)
        ranks = []
        for b in range(4):
            block = named[:, b * 256 : (b + 1) * 256]
            count = dot(block.astype(BF16), before) + carry
            ranks.append(jnp.sum(block * count, axis=0, keepdims=True))
            carry = carry + jnp.sum(block, axis=1, keepdims=True)
        key_ref[...] = owner * 256 + jnp.concatenate(ranks, axis=1).astype(I32)
        row = row_ref[...]
        which = iota((E, 4 * SAMPLES), 0)
        parts = jnp.where(which == 0, row // 128, jnp.where(which == 1, row % 128, 0))
        gext_ref[:, E:] = parts.astype(F32).T.astype(BF16)

    @pl.when(step > 0)
    def _():
        acc[...] += part

    @pl.when(step == pl.num_programs(0) - 1)
    def _():
        for f in range(HOT_FIELDS):
            hotg_ref[f] = acc[:, f * E : (f + 1) * E].astype(BF16)
        for f in range(COLD_FIELDS):
            cold[pl.ds(f, SAMPLES, stride=COLD_FIELDS), :] = acc[:, (HOT_FIELDS + f) * E : (HOT_FIELDS + f + 1) * E]
        gext_ref[:, :E] = cold[...].astype(BF16)


def grads(features, w_in, upstream, hot_ids, cold_rows, owners):
    lookups = SAMPLES * COLD_FIELDS
    fixed = lambda shape: pl.BlockSpec(shape, lambda j: (0,) * len(shape))
    return pl.pallas_call(
        grads_kernel,
        grid=(w_in.shape[1] // STEP,),
        in_specs=[
            fixed(features.shape),
            pl.BlockSpec((w_in.shape[0], STEP), lambda j: (0, j)),
            pl.BlockSpec((SAMPLES, STEP), lambda j: (0, j)),
            fixed(hot_ids.shape),
            fixed((1, lookups)),
            fixed((1, lookups)),
        ],
        out_specs=[
            fixed((HOT_FIELDS, SAMPLES, E)),
            fixed((lookups, 2 * E)),
            fixed((1, lookups)),
            fixed((HOT_FIELDS, SAMPLES)),
        ],
        out_shape=[
            jax.ShapeDtypeStruct((HOT_FIELDS, SAMPLES, E), BF16),
            jax.ShapeDtypeStruct((lookups, 2 * E), BF16),
            jax.ShapeDtypeStruct((1, lookups), I32),
            jax.ShapeDtypeStruct((HOT_FIELDS, SAMPLES), I32),
        ],
        scratch_shapes=[pltpu.VMEM((SAMPLES, w_in.shape[0]), F32), pltpu.VMEM((lookups, E), F32)],
        compiler_params=pltpu.CompilerParams(vmem_limit_bytes=40 << 20),
        name="grads",
    )(features, w_in, upstream, hot_ids, cold_rows, owners)


def sums_kernel(
    gext_ref, key_ref, hotg_ref, hid_ref, cold_ref, hot_ref,
    csend, crecv, hotg2, hid2, hacc, xsend, xrecv, ysend, yown, yrecv, zsend, zrecv, grecv,
    c_ss, c_rs, h_ss, h_rs, x_ss, x_rs, y_ss, y_rs, z_ss, z_rs, g_ss, g_rs,
):
    g, s = lax.axis_index("grp"), lax.axis_index("shard")
    zl, y = g // 8, g % 8
    zh, x, c = s // 8, (s // 2) % 4, s % 2
    z = zh * 4 + zl

    def at(zh, x, c):
        return (zh * 4 + x) * 2 + c

    def cold_peer(k):
        return at((zh + k // 8) % 3, (x + (k // 2) % 4) % 4, (c + k % 2) % 2)

    def y_peer(d):
        return (zl * 8 + (y + d) % 8, s)

    def z_peer(d):
        to = (z + d) % 12
        return ((to % 4) * 8 + y, at(to // 4, x, c))

    def copy(src, dst, ss, rs, peer):
        return pltpu.make_async_remote_copy(
            src_ref=src, dst_ref=dst, send_sem=ss, recv_sem=rs, device_id=peer, device_id_type=MESH
        )

    def cold_copy(k):
        return copy(csend.at[k], crecv.at[k, pl.ds(0, SLOTS)], c_ss.at[k], c_rs.at[k], (g, cold_peer(k)))

    def x_copy(d):
        return copy(xsend.at[d], xrecv.at[d], x_ss.at[d], x_rs.at[d], (g, at(zh, (x + d) % 4, c)))

    def y_copy(d):
        return copy(ysend.at[d], yrecv.at[d], y_ss.at[d], y_rs.at[d], y_peer(d))

    def z_copy(d):
        return copy(zsend.at[((z + d) % 12) // 4], zrecv.at[z], z_ss.at[d], z_rs.at[d], z_peer(d))

    def g_copy(d):
        return copy(grecv.at[y], grecv.at[y], g_ss.at[d], g_rs.at[d], y_peer(d))

    barrier = pltpu.get_barrier_semaphore()

    def greet(peer):
        pl.semaphore_signal(barrier, inc=1, device_id=peer, device_id_type=MESH)

    for k in range(1, OWNERS):
        greet((g, cold_peer(k)))
    for d in range(1, 8):
        greet(y_peer(d))
    for d in range(1, 12):
        if d not in (4, 8):
            greet(z_peer(d))

    which = iota((8, E), 0)
    column = iota((8, E), 1)
    pick = jnp.where(
        ((which == 2) | (which == 3)) & (column == 0) | ((which == 4) | (which == 5)) & (column == 1), 1.0, 0.0
    ).astype(BF16)

    def place(k, carry):
        slot = key_ref[...] - cold_peer(k) * 256
        chosen = (slot == iota((SLOTS, slot.shape[1]), 0)).astype(BF16)
        rows = dot(chosen, gext_ref[...])
        numbers = jnp.concatenate([rows[:, E:], jnp.zeros((DEPTH - SLOTS, E), F32)], axis=0).astype(BF16)
        numbers = nt_dot(pick, numbers)
        tail = jnp.where((which == 2) | (which == 4), numbers[:, :E], numbers[:, E:])
        csend[k] = jnp.concatenate([rows[:HEAD, :E], rows[HEAD:, :E] + tail], axis=0).astype(BF16)
        crecv[k, SLOTS:, :] = jnp.zeros((DEPTH - SLOTS, E), BF16)
        return carry

    lax.fori_loop(0, OWNERS, place, 0)
    crecv[0, :SLOTS, :] = csend[0]
    cold_ref[...] = jnp.zeros_like(cold_ref)
    pl.semaphore_wait(barrier, OWNERS - 1 + 7 + 9)

    hot_pair = copy(hotg_ref, hotg2, h_ss.at[0], h_rs.at[0], (g, at(zh, x, 1 - c)))
    ids_pair = copy(hid_ref, hid2, h_ss.at[1], h_rs.at[1], (g, at(zh, x, 1 - c)))
    ids_pair.start()
    hot_pair.start()

    def send_far(i, carry):
        cold_copy(8 * (1 + i % 2) + i // 2).start()
        return carry

    lax.fori_loop(0, 16, send_far, 0)

    def send_near(k, carry):
        cold_copy(k).start()
        return carry

    lax.fori_loop(1, 8, send_near, 0)

    def hot_block(i, ids_ref, rows_ref):
        base = at(i % 3, (x + i // 3) % 4, c) * 256
        total = jnp.zeros((256, E), F32)
        for f in range(HOT_FIELDS):
            named = (ids_ref[f : f + 1, :] - base == iota((256, SAMPLES), 0)).astype(BF16)
            total = total + dot(named, rows_ref[f])
        return total

    def hot_mine(i, carry):
        hacc[i] = hot_block(i, hid_ref, hotg_ref)
        return carry

    lax.fori_loop(0, 12, hot_mine, 0)
    ids_pair.wait_recv()
    hot_pair.wait_recv()

    def hot_theirs(i, carry):
        xsend[i // 3, pl.ds((i % 3) * 256, 256), :] = (hacc[i] + hot_block(i, hid2, hotg2)).astype(BF16)
        return carry

    for d in (1, 3, 2):
        lax.fori_loop(3 * d, 3 * d + 3, hot_theirs, 0)
        x_copy(d).start()

    def hot_own(i, carry):
        hacc[i] = hacc[i] + hot_block(i, hid2, hotg2)
        return carry

    lax.fori_loop(0, 3, hot_own, 0)

    def cold_add(k, carry):
        tile = crecv[k, SLOTS - 16 : SLOTS, :].astype(F32)
        low = tile[10:11] * 128.0 + tile[12:13]
        high = jnp.where(iota((1, E), 1) < USED - 128, tile[11:12] * 128.0 + tile[13:14], -1.0)
        ids = jnp.concatenate([low, high], axis=1).astype(I32)
        rows = crecv[k]
        for b in range(OWNED // 256):
            named = (ids - b * 256 == iota((256, DEPTH), 0)).astype(BF16)
            cold_ref[b * 256 : (b + 1) * 256, :] += dot(named, rows)
        return carry

    def cold_arrived(k, carry):
        cold_copy(k).wait_recv()
        return cold_add(k, carry)

    cold_add(0, 0)
    lax.fori_loop(1, 8, cold_arrived, 0)

    for d in (1, 3, 2):
        x_copy(d).wait_recv()

    def over_x(i, carry):
        rows = pl.ds(i * 256, 256)
        total = hacc[i]
        for d in range(1, 4):
            total = total + xrecv[d, rows, :].astype(F32)
        hacc[i] = total
        return carry

    lax.fori_loop(0, 3, over_x, 0)

    def to_y(d, carry):
        rows = pl.ds(pl.multiple_of(((y + d) % 8) * 32, 32), 32)
        for i in range(3):
            ysend[d, i * 32 : (i + 1) * 32, :] = hacc[i, rows, :].astype(BF16)
        y_copy(d).start()
        return carry

    lax.fori_loop(1, 8, to_y, 0)
    mine = pl.ds(pl.multiple_of(y * 32, 32), 32)
    for i in range(3):
        yown[i] = hacc[i, mine, :]

    lax.fori_loop(8, 14, cold_arrived, 0)

    for d in range(1, 8):
        y_copy(d).wait_recv()
    for i in range(3):
        total = yown[i]
        for d in range(1, 8):
            total = total + yrecv[d, i * 32 : (i + 1) * 32, :].astype(F32)
        zsend[i] = total
    zrecv[z] = zsend[zh]
    for d in range(1, 12):
        z_copy(d).start()

    lax.fori_loop(14, 19, cold_arrived, 0)

    for d in range(1, 12):
        copy(zsend.at[zh], zrecv.at[(z + 12 - d) % 12], z_ss.at[d], z_rs.at[d], z_peer(d)).wait_recv()
    total = zrecv[0]
    for i in range(1, 12):
        total = total + zrecv[i]
    grecv[y] = total
    for d in range(1, 8):
        g_copy(d).start()

    lax.fori_loop(19, OWNERS, cold_arrived, 0)

    for d in range(1, 8):
        copy(grecv.at[y], grecv.at[(y + 8 - d) % 8], g_ss.at[d], g_rs.at[d], y_peer(d)).wait_recv()
    for i in range(8):
        hot_ref[i * 32 : (i + 1) * 32, :] = grecv[i]

    def cold_sent(k, carry):
        cold_copy(k).wait_send()
        return carry

    lax.fori_loop(1, OWNERS, cold_sent, 0)
    ids_pair.wait_send()
    hot_pair.wait_send()
    for d in range(1, 4):
        x_copy(d).wait_send()
    for d in range(1, 8):
        y_copy(d).wait_send()
        g_copy(d).wait_send()
    for d in range(1, 12):
        z_copy(d).wait_send()


def sums(gext, key, hotg, hid):
    vmem = pl.BlockSpec(memory_space=pltpu.VMEM)
    dma = pltpu.SemaphoreType.DMA
    pairs = lambda n: [dma((n,)), dma((n,))]
    return pl.pallas_call(
        sums_kernel,
        in_specs=[vmem] * 4,
        out_specs=[vmem] * 2,
        out_shape=[jax.ShapeDtypeStruct((OWNED, E), F32), jax.ShapeDtypeStruct((256, E), F32)],
        scratch_shapes=[
            pltpu.VMEM((OWNERS, SLOTS, E), BF16),
            pltpu.VMEM((OWNERS, DEPTH, E), BF16),
            pltpu.VMEM((HOT_FIELDS, SAMPLES, E), BF16),
            pltpu.VMEM((HOT_FIELDS, SAMPLES), I32),
            pltpu.VMEM((12, 256, E), F32),
            pltpu.VMEM((4, 768, E), BF16),
            pltpu.VMEM((4, 768, E), BF16),
            pltpu.VMEM((8, 96, E), BF16),
            pltpu.VMEM((3, 32, E), F32),
            pltpu.VMEM((8, 96, E), BF16),
            pltpu.VMEM((3, 32, E), F32),
            pltpu.VMEM((12, 32, E), F32),
            pltpu.VMEM((8, 32, E), F32),
        ]
        + pairs(OWNERS) + pairs(2) + pairs(4) + pairs(8) + pairs(12) + pairs(8),
        compiler_params=pltpu.CompilerParams(
            collective_id=0, has_side_effects=True, vmem_limit_bytes=40 << 20
        ),
        name="sums",
    )(gext, key, hotg, hid)


def adagrad(rows, accum, grads):
    accum_new = accum + jnp.mean(grads * grads, axis=1)
    return (rows - learn_rate * grads / jnp.sqrt(accum_new)[:, None], accum_new)


def shards(
    features,
    w_in,
    upstream,
    hot_ids,
    cold_rows,
    cold_owner,
    hot_table,
    hot_accum,
    cold_table,
    cold_accum,
):
    hotg, gext, key, hid = grads(
        features, w_in, upstream, hot_ids, cold_rows.reshape(1, -1), cold_owner.reshape(1, -1)
    )
    cold_sum, hot_sum = sums(gext, key, hotg, hid)
    hot_new, hot_accum_new = adagrad(hot_table, hot_accum, hot_sum)
    cold_new, cold_accum_new = adagrad(cold_table, cold_accum, cold_sum)
    return (hot_new, hot_accum_new, cold_new, cold_accum_new)


def solution(mesh):
    placed = (
        P(("grp", "shard"), None),
        P(),
        P(("grp", "shard"), None),
        P(("grp", "shard"), None),
        P(("grp", "shard")),
        P(("grp", "shard"), None),
        P("shard", None),
        P("shard"),
        P(("grp", "shard"), None),
        P(("grp", "shard")),
    )
    return jax.shard_map(
        shards,
        mesh=mesh,
        in_specs=placed,
        out_specs=(P("shard", None), P("shard"), P(("grp", "shard"), None), P(("grp", "shard"))),
        check_vma=False,
    )
```

time: 487 us -> 93.2 us (0.19)
  waiting for transfers between devices: 374 us -> 0 us
  Pallas kernels: 0 us -> 82.2 us
  other arithmetic: 54.1 us -> 3.7 us
  starting transfers between devices: 24.9 us -> 0 us
  between operations: 14.3 us -> 0.71 us
  local copies, waits for them, and re-layouts: 13.3 us -> 6.27 us
  matrix products: 5.88 us -> 0 us
    psum x1 -> x0, waiting for transfers between devices: 283 us -> none  [shards(): total = lax.psum(mine, 'grp')]
    pallas_call x0 -> x2, Pallas kernels: none -> 82.2 us  [the longest x1 76.6 us: sums(): pl.pallas_call(sums_kernel, in_specs=[vmem] * 4, out_specs=[vmem] * 2, ou...]
    all_to_all x2 -> x0, waiting for transfers between devices: 48.2 us -> none  [the longest x1 46.2 us: shards(): lax.all_to_all(outgoing, 'shard', split_axis=0, concat_axis=0, tiled=True)]
    reduce_scatter x1 -> x0, waiting for transfers between devices: 43.4 us -> none  [shards(): lax.psum_scatter(partial_value, 'shard', scatter_dimension=0, tiled=True)]
    scatter-add x2 -> x0, other arithmetic: 41.4 us -> none  [the longest x1 28.1 us: shards(): jax.ops.segment_sum(arrived.reshape(-1, width).astype(jnp.float32), arriv...]
    all_to_all x2 -> x0, starting transfers between devices: 24.6 us -> none  [the longest x1 17 us: shards(): lax.all_to_all(outgoing_ids, 'shard', split_axis=0, concat_axis=0, tiled=...]
    another operation x2 -> x0, other arithmetic: 6.8 us -> none
    dot_general x3 -> x0, matrix products: 5.88 us -> none  [the longest x1 3.4 us: shards(): preact = jnp.dot(features, w_in, preferred_element_type=jnp.float32)]
  transfers between devices with their start and end apart: 4 -> 0, of which waited for: 4 -> 0; matrix products, arithmetic and copies ran while one was open for 10% -> 0% of each run, Pallas kernels for 0% -> 0%
where the time goes in v1:
time: 93.2 us; the launch traced here: 92.9 us
  Pallas kernels  82.2 us (88%)
  local copies, waits for them, and re-layouts  6.27 us (7%)
  other arithmetic  3.7 us (4%)
    pallas_call x1, Pallas kernels, sums(): pl.pallas_call(sums_kernel, in_specs=[vmem] * 4, out_specs=[vmem] * 2, ou...  76.6 us
    unnamed x19, local copies, waits for them, and re-layouts  6.27 us
    pallas_call x1, Pallas kernels, grads(): pl.pallas_call(grads_kernel, grid=(w_in.shape[1] // STEP,), in_specs=[fix...  5.57 us
    sub x2, other arithmetic, adagrad(): return (rows - learn_rate * grads / jnp.sqrt(accum_new)[:, None], accum_new)  2.08 us

profile of v1, /device:TPU:2, one launch (start us, length us, event | category | flops | bytes accessed | tf_op | source)
XLA Modules:
  0.0 92.9 jit_solution(322001229853472536)
XLA Ops:
  0.6 0.8 copy.14.hid_ref
  1.5 0.0 copy-start
  1.5 1.9 %copy-done = bf16[1536,1024]{1,0:T(8,128)(2,1)S(1)} copy-done((bf16[1536,1024]{1,0:T(8,128)(2,1)S(1)}, bf16[1536,1024]{1,0:T(8,128)(2,1)}, u32[]{:S(2)}) %copy-start) | copy-done | bytes 3145752
  3.4 0.0 copy-start.1
  3.4 1.1 %copy-done.1 = bf16[256,1536]{1,0:T(8,128)(2,1)S(1)} copy-done((bf16[256,1536]{1,0:T(8,128)(2,1)S(1)}, bf16[256,1536]{1,0:T(8,128)(2,1)}, u32[]{:S(2)}) %copy-start.1) | copy-done | bytes 786456
  4.5 0.0 copy-start.2
  4.5 1.0 %copy-done.2 = bf16[256,1024]{1,0:T(8,128)(2,1)S(1)} copy-done((bf16[256,1024]{1,0:T(8,128)(2,1)S(1)}, bf16[256,1024]{1,0:T(8,128)(2,1)}, u32[]{:S(2)}) %copy-start.2) | copy-done | bytes 524312
  5.5 0.0 copy-start.3
  5.5 0.7 copy-done.3
  6.2 0.0 copy-start.4
  6.2 0.7 copy-done.4
  6.9 0.0 copy-start.7
  6.9 0.0 copy-start.5
  6.9 5.6 %grads.1 = (bf16[8,256,128]{2,1,0:T(8,128)(2,1)S(1)}, bf16[1024,256]{1,0:T(8,128)(2,1)S(1)}, s32[1,1024]{1,0:T(1,128)S(1)}, s32[8,256]{1,0:T(8,128)S(1)}) custom-call(bf16[256,1536]{1,0:T(8,128)(2,1)S(1)} %copy-done.1, bf16[1536,1024]{1,0:T(8,128)(2,1)S(1)} %copy-done, bf16[256,1024]{1,0:T(8,128)(2,1)S(1)} %copy-done.2, s32[256,8]{1,0:T(8,128)S(1)} %copy.14.hid_ref, ...), custom_call_target="tpu_custom_call" | custom-call | tf_op jit(solution)/shard_map/grads/pallas_call | solution.py:82
  12.5 0.0 copy-start.8
  12.5 0.0 copy-start.6
  12.5 76.6 %sums.1 = (f32[2048,128]{1,0:T(8,128)S(1)}, f32[256,128]{1,0:T(8,128)S(1)}) custom-call(bf16[1024,256]{1,0:T(8,128)(2,1)S(1)} %get-tuple-element.10.gext_ref, s32[1,1024]{1,0:T(1,128)S(1)} %get-tuple-element.11.key_ref, bf16[8,256,128]{2,1,0:T(8,128)(2,1)S(1)} %get-tuple-element.12.hotg_ref, s32[8,256]{1,0:T(8,128)S(1)} %get-tuple-element.13.hid_ref), custom_call_target="tpu_custom_call" | custom-call | tf_op jit(solution)/shard_map/sums/pallas_call | solution.py:330
  89.1 0.3 multiply_reduce_fusion
  89.5 0.0 copy-done.7
  89.5 0.6 fusion
  90.1 0.0 copy-done.5
  90.1 1.3 %divide_subtract_fusion = f32[2048,128]{1,0:T(8,128)} fusion(f32[2048,128]{1,0:T(8,128)S(1)} %copy-done.5, f32[2048,128]{1,0:T(8,128)S(1)} %get-tuple-element.15, f32[2048]{0:T(1024)S(1)} %get-tuple-element.16), kind=kLoop, calls=%fused_computation | loop fusion | flops 786432 | bytes 3153920 | tf_op jit(solution)/shard_map/sub | solution.py:360
  91.4 0.1 multiply_reduce_fusion.1
  91.5 0.0 copy-done.8
  91.5 0.6 fusion.1
  92.1 0.0 copy-done.6
  92.1 0.8 divide_subtract_fusion.1
Async XLA Ops:
  1.5 1.9 %copy-start = (bf16[1536,1024]{1,0:T(8,128)(2,1)S(1)}, bf16[1536,1024]{1,0:T(8,128)(2,1)}, u32[]{:S(2)}) copy-start(bf16[1536,1024]{1,0:T(8,128)(2,1)} %w_ref.1) | copy-start | bytes 9437188
  3.4 1.1 %copy-start.1 = (bf16[256,1536]{1,0:T(8,128)(2,1)S(1)}, bf16[256,1536]{1,0:T(8,128)(2,1)}, u32[]{:S(2)}) copy-start(bf16[256,1536]{1,0:T(8,128)(2,1)} %feat_ref.1) | copy-start | bytes 2359300
  4.5 1.0 %copy-start.2 = (bf16[256,1024]{1,0:T(8,128)(2,1)S(1)}, bf16[256,1024]{1,0:T(8,128)(2,1)}, u32[]{:S(2)}) copy-start(bf16[256,1024]{1,0:T(8,128)(2,1)} %up_ref.1) | copy-start | bytes 1572868
  5.5 0.7 copy-start.3
  6.2 0.7 copy-start.4
  6.9 82.6 %copy-start.7 = (f32[2048]{0:T(1024)S(1)}, f32[2048]{0:T(1024)}, u32[]{:S(2)}) copy-start(f32[2048]{0:T(1024)} %param.19) | copy-start | bytes 24580
  6.9 83.2 %copy-start.5 = (f32[2048,128]{1,0:T(8,128)S(1)}, f32[2048,128]{1,0:T(8,128)}, u32[]{:S(2)}) copy-start(f32[2048,128]{1,0:T(8,128)} %param.18) | copy-start | bytes 3145732
  12.5 79.0 %copy-start.8 = (f32[256]{0:T(256)S(1)}, f32[256]{0:T(256)}, u32[]{:S(2)}) copy-start(f32[256]{0:T(256)} %param.17) | copy-start | bytes 3076
  12.5 79.6 %copy-start.6 = (f32[256,128]{1,0:T(8,128)S(1)}, f32[256,128]{1,0:T(8,128)}, u32[]{:S(2)}) copy-start(f32[256,128]{1,0:T(8,128)} %param.16) | copy-start | bytes 393220

commit v2 on v0

v2 whole, which is shorter than its diff:
```python
import jax
import jax.numpy as jnp
from jax import lax
from jax.experimental import pallas as pl
from jax.experimental.pallas import tpu as pltpu
from jax.sharding import PartitionSpec as P

MESH = pl.DeviceIdType.MESH
learn_rate = 0.5

E = 128
SAMPLES = 256
HOT_FIELDS, COLD_FIELDS = 8, 4
PLANE = 8
LOOKUPS = 1024
SLOTS = 176
USED = 170
HEAD = 168
DEPTH = 256
OWNED = 2048
STEP = 256
STEPS = 4
BF16, F32, I32 = jnp.bfloat16, jnp.float32, jnp.int32


def iota(shape, axis):
    return lax.broadcasted_iota(I32, shape, axis)


def nt_dot(a, b):
    return lax.dot_general(a, b, (((1,), (1,)), ((), ())), preferred_element_type=F32)


def dot(a, b):
    return jnp.dot(a, b, preferred_element_type=F32)


def step_kernel(
    feat_hbm, w_hbm, up_hbm, hid_ref, row_ref, own_ref, cold_ref, hot_ref,
    feat, w, up, delta, hotg, hotg2, hid2, wide, hacc, xsend, xrecv, ysend, yown, yrecv, zsend, zrecv, grecv,
    raw, packed, loose, csend, crecv,
    l_s, r_ss, r_rs, p_ss, p_rs, c_ss, c_rs, h_ss, h_rs, x_ss, x_rs, y_ss, y_rs, z_ss, z_rs, g_ss, g_rs,
):
    g, s = lax.axis_index("grp"), lax.axis_index("shard")
    zl, y = g // 8, g % 8
    zh, x, c = s // 8, (s // 2) % 4, s % 2
    z = zh * 4 + zl

    def at(zh, x, c):
        return (zh * 4 + x) * 2 + c

    def plane_peer(k):
        return (g, at(zh, (x + k // 2) % 4, (c + k % 2) % 2))

    def y_peer(d):
        return (zl * 8 + (y + d) % 8, s)

    def z_peer(d):
        to = (z + d) % 12
        return ((to % 4) * 8 + y, at(to // 4, x, c))

    def copy(src, dst, ss, rs, peer):
        return pltpu.make_async_remote_copy(
            src_ref=src, dst_ref=dst, send_sem=ss, recv_sem=rs, device_id=peer, device_id_type=MESH
        )

    def raw_copy(q):
        return copy(raw.at[0], raw.at[q], r_ss.at[q], r_rs.at[q], (g, at((zh + q) % 3, x, c)))

    def packed_copy(q):
        return copy(packed.at[0], packed.at[q], p_ss.at[q], p_rs.at[q], (g, at((zh + q) % 3, x, c)))

    def cold_copy(q, k):
        return copy(
            csend.at[q, k], crecv.at[q, k, pl.ds(0, SLOTS)], c_ss.at[q, k], c_rs.at[q, k], plane_peer(k)
        )

    def pair_copy(i):
        return copy(
            hotg.at[pl.ds(2 * i, 2)], hotg2.at[pl.ds(2 * i, 2)], h_ss.at[i], h_rs.at[i], plane_peer(1)
        )

    ids_copy = copy(hid_ref, hid2, h_ss.at[4], h_rs.at[4], plane_peer(1))

    def x_copy(d):
        return copy(xsend.at[d], xrecv.at[d], x_ss.at[d], x_rs.at[d], plane_peer(2 * d))

    def y_copy(d):
        return copy(ysend.at[d], yrecv.at[d], y_ss.at[d], y_rs.at[d], y_peer(d))

    def z_copy(d):
        return copy(zsend.at[((z + d) % 12) // 4], zrecv.at[z], z_ss.at[d], z_rs.at[d], z_peer(d))

    def g_copy(d):
        return copy(grecv.at[y], grecv.at[y], g_ss.at[d], g_rs.at[d], y_peer(d))

    barrier = pltpu.get_barrier_semaphore()

    def greet(peer):
        pl.semaphore_signal(barrier, inc=1, device_id=peer, device_id_type=MESH)

    for d in (4, 8, 1, 2, 3, 5, 6, 7, 9, 10, 11):
        greet(z_peer(d))
    for k in range(1, PLANE):
        greet(plane_peer(k))
    for d in range(1, 8):
        greet(y_peer(d))

    feat_copy = pltpu.make_async_copy(feat_hbm, feat, l_s.at[STEPS])
    up_copy = pltpu.make_async_copy(up_hbm, up, l_s.at[STEPS + 1])

    def w_copy(j):
        columns = pl.ds(pl.multiple_of(j * STEP, STEP), STEP)
        return pltpu.make_async_copy(w_hbm.at[:, columns], w.at[j], l_s.at[j])

    feat_copy.start()
    w_copy(0).start()
    up_copy.start()
    for j in range(1, STEPS):
        w_copy(j).start()

    owner = own_ref[...]
    named = (owner == iota((32, LOOKUPS), 0)).astype(F32)
    before = (iota((256, 256), 0) < iota((256, 256), 1)).astype(BF16)
    carry = jnp.zeros((32, 1), F32)
    ranks = []
    for b in range(LOOKUPS // 256):
        block = named[:, b * 256 : (b + 1) * 256]
        count = dot(block.astype(BF16), before) + carry
        ranks.append(jnp.sum(block * count, axis=0, keepdims=True))
        carry = carry + jnp.sum(block, axis=1, keepdims=True)
    packed[0] = (owner * 256 + jnp.concatenate(ranks, axis=1).astype(I32)) * OWNED + row_ref[...]
    crecv[:, :, SLOTS:, :] = jnp.zeros((3, PLANE, DEPTH - SLOTS, E), BF16)
    cold_ref[...] = jnp.zeros_like(cold_ref)
    hacc[...] = jnp.zeros_like(hacc)

    feat_copy.wait()

    def grad_step(j, total):
        w_copy(j).wait()
        preact = dot(feat[...], w[j])
        sigm = jax.nn.sigmoid(preact)
        part = (up[:, pl.ds(pl.multiple_of(j * STEP, STEP), STEP)].astype(F32) * sigm * (1.0 + preact * (1.0 - sigm))).astype(BF16)
        delta[j] = part
        return total + nt_dot(part, w[j, HOT_FIELDS * E :, :])

    up_copy.wait()
    total = lax.fori_loop(0, STEPS, grad_step, jnp.zeros((SAMPLES, COLD_FIELDS * E), F32))
    for f in range(COLD_FIELDS):
        loose[pl.ds(f, SAMPLES, stride=COLD_FIELDS), :] = total[:, f * E : (f + 1) * E]
    raw[0] = loose[...].astype(BF16)

    pl.semaphore_wait(barrier, 11 + 7 + 7)
    for q in (1, 2):
        raw_copy(q).start()
        packed_copy(q).start()
    ids_copy.start()

    def hot_step(i, carry):
        rows = pl.ds(pl.multiple_of(i * 2 * E, 2 * E), 2 * E)
        total = nt_dot(delta[0], w[0, rows, :])
        for j in range(1, STEPS):
            total = total + nt_dot(delta[j], w[j, rows, :])
        hotg[2 * i] = total[:, :E].astype(BF16)
        hotg[2 * i + 1] = total[:, E:].astype(BF16)
        pair_copy(i).start()
        return carry

    lax.fori_loop(0, HOT_FIELDS // 2, hot_step, 0)

    def hot_add(ids_ref, rows_ref, parity):
        ids = ids_ref[...]
        place = ids // 256
        away = ((place // 2) % 4 - x + 4) % 4
        inside = (place % 2 == c) & (away % 2 == parity)
        spot = jnp.where(inside, place // 8 * 256 + ids % 256, -1)
        for i in range(HOT_FIELDS // 2):
            chosen = jnp.concatenate(
                [(spot[2 * i + n : 2 * i + n + 1, :] == iota((768, SAMPLES), 0)).astype(BF16) for n in range(2)], axis=1
            )
            hacc[parity] += dot(chosen, rows_ref[2 * i * SAMPLES : (2 * i + 2) * SAMPLES, :])

    def widen(ids_ref, rows_ref):
        far = ((ids_ref[...] // 512) % 4 - x + 4) % 4 // 2
        far = far.astype(F32).T
        for f in range(HOT_FIELDS):
            keep = jnp.broadcast_to(far[:, f : f + 1], (SAMPLES, E)).astype(BF16)
            rows = rows_ref[f]
            second = rows * keep
            wide[f * SAMPLES : (f + 1) * SAMPLES, :E] = rows - second
            wide[f * SAMPLES : (f + 1) * SAMPLES, E:] = second

    widen(hid_ref, hotg)
    hot_add(hid_ref, wide, 1)
    hot_add(hid_ref, wide, 0)
    ids_copy.wait_recv()
    for i in range(HOT_FIELDS // 2):
        pair_copy(i).wait_recv()
    widen(hid2, hotg2)
    hot_add(hid2, wide, 1)
    xsend[1] = hacc[1, :, :E].astype(BF16)
    x_copy(1).start()
    xsend[3] = hacc[1, :, E:].astype(BF16)
    x_copy(3).start()
    hot_add(hid2, wide, 0)
    xsend[2] = hacc[0, :, E:].astype(BF16)
    x_copy(2).start()

    which = iota((8, E), 0)
    column = iota((8, E), 1)
    pick = jnp.where(
        ((which == 2) | (which == 3)) & (column == 0) | ((which == 4) | (which == 5)) & (column == 1), 1.0, 0.0
    ).astype(BF16)

    def place(q):
        both = packed[q]
        slot, row = both // OWNED, both % OWNED
        sort = iota((E, LOOKUPS), 0)
        parts = jnp.where(sort == 0, row // 128, jnp.where(sort == 1, row % 128, 0)).astype(F32).T
        rows = jnp.concatenate([raw[q], parts.astype(BF16)], axis=1)

        def pair(dx):
            base = slot - at(zh, (x + dx) % 4, 0) * 256
            chosen = jnp.concatenate(
                [(base - n * 256 == iota((SLOTS, LOOKUPS), 0)).astype(BF16) for n in range(2)], axis=0
            )
            placed = dot(chosen, rows)
            for n in range(2):
                half = placed[n * SLOTS : (n + 1) * SLOTS]
                numbers = jnp.concatenate([half[:, E:], jnp.zeros((DEPTH - SLOTS, E), F32)], axis=0).astype(BF16)
                numbers = nt_dot(pick, numbers)
                tail = jnp.where((which == 2) | (which == 4), numbers[:, :E], numbers[:, E:])
                k = 2 * dx + (n + c) % 2
                csend[q, k] = jnp.concatenate([half[:HEAD, :E], half[HEAD:, :E] + tail], axis=0).astype(BF16)

        def far(dx, carry):
            pair(dx)
            cold_copy(q, 2 * dx).start()
            cold_copy(q, 2 * dx + 1).start()
            return carry

        lax.fori_loop(1, 4, far, 0)
        pair(0)
        cold_copy(q, 1).start()
        crecv[q, 0, :SLOTS, :] = csend[q, 0]

    def cold_add(q, ks):
        ids, rows = [], []
        for k in ks:
            tile = crecv[q, k, SLOTS - 16 : SLOTS, :].astype(F32)
            low = tile[10:11] * 128.0 + tile[12:13]
            high = jnp.where(iota((1, E), 1) < USED - 128, tile[11:12] * 128.0 + tile[13:14], -1.0)
            number = jnp.concatenate([low, high], axis=1)
            far = jnp.broadcast_to((number >= OWNED // 2).astype(F32), (8, DEPTH)).T
            keep = jnp.broadcast_to(far[:, :1], (DEPTH, E)).astype(BF16)
            arrived = crecv[q, k]
            second = arrived * keep
            rows.append(jnp.concatenate([arrived - second, second], axis=1))
            ids.append(number.astype(I32))
        ids, rows = jnp.concatenate(ids, axis=1), jnp.concatenate(rows, axis=0)
        ids = jnp.where(ids < 0, -1, ids % (OWNED // 2))
        for b in range(OWNED // 512):
            chosen = (ids - b * 256 == iota((256, ids.shape[1]), 0)).astype(BF16)
            total = dot(chosen, rows)
            cold_ref[b * 256 : (b + 1) * 256, :] += total[:, :E]
            cold_ref[OWNED // 2 + b * 256 : OWNED // 2 + (b + 1) * 256, :] += total[:, E:]

    def cold_arrived(q):
        def step(i, carry):
            cold_copy(q, 2 * i).wait_recv()
            cold_copy(q, 2 * i + 1).wait_recv()
            cold_add(q, (2 * i, 2 * i + 1))
            return carry

        cold_copy(q, 1).wait_recv()
        cold_add(q, (0, 1))
        lax.fori_loop(1, 4, step, 0)

    place(0)

    for d in (1, 3, 2):
        x_copy(d).wait_recv()

    def over_x(i, carry):
        rows = pl.ds(pl.multiple_of(i * 256, 256), 256)
        total = hacc[0, rows, :E]
        for d in range(1, 4):
            total = total + xrecv[d, rows, :].astype(F32)
        hacc[0, rows, :E] = total
        return carry

    lax.fori_loop(0, 3, over_x, 0)

    def to_y(d, carry):
        for i in range(3):
            rows = pl.ds(pl.multiple_of(((y + d) % 8) * 32 + i * 256, 32), 32)
            ysend[d, i * 32 : (i + 1) * 32, :] = hacc[0, rows, :E].astype(BF16)
        y_copy(d).start()
        return carry

    lax.fori_loop(1, 8, to_y, 0)
    for i in range(3):
        yown[i] = hacc[0, pl.ds(pl.multiple_of(y * 32 + i * 256, 32), 32), :E]

    cold_arrived(0)

    for d in range(1, 8):
        y_copy(d).wait_recv()
    for i in range(3):
        total = yown[i]
        for d in range(1, 8):
            total = total + yrecv[d, i * 32 : (i + 1) * 32, :].astype(F32)
        zsend[i] = total
    zrecv[z] = zsend[zh]
    for d in range(1, 12):
        z_copy(d).start()

    for q in (1, 2):
        packed_copy(q).wait_recv()
        raw_copy(q).wait_recv()
        place(q)

    for d in range(1, 12):
        copy(zsend.at[zh], zrecv.at[(z + 12 - d) % 12], z_ss.at[d], z_rs.at[d], z_peer(d)).wait_recv()
    total = zrecv[0]
    for i in range(1, 12):
        total = total + zrecv[i]
    grecv[y] = total
    for d in range(1, 8):
        g_copy(d).start()

    cold_arrived(1)
    cold_arrived(2)

    for d in range(1, 8):
        copy(grecv.at[y], grecv.at[(y + 8 - d) % 8], g_ss.at[d], g_rs.at[d], y_peer(d)).wait_recv()
    for i in range(8):
        hot_ref[i * 32 : (i + 1) * 32, :] = grecv[i]

    for q in (1, 2):
        raw_copy(q).wait_send()
        packed_copy(q).wait_send()
    ids_copy.wait_send()
    for i in range(HOT_FIELDS // 2):
        pair_copy(i).wait_send()

    def cold_sent(k, carry):
        for q in range(3):
            cold_copy(q, k).wait_send()
        return carry

    lax.fori_loop(1, PLANE, cold_sent, 0)
    for d in range(1, 4):
        x_copy(d).wait_send()
    for d in range(1, 8):
        y_copy(d).wait_send()
        g_copy(d).wait_send()
    for d in range(1, 12):
        z_copy(d).wait_send()


def step(features, w_in, upstream, hot_ids, cold_rows, owners):
    vmem = pl.BlockSpec(memory_space=pltpu.VMEM)
    hbm = pl.BlockSpec(memory_space=pl.ANY)
    dma = pltpu.SemaphoreType.DMA
    pairs = lambda *n: [dma(n), dma(n)]
    return pl.pallas_call(
        step_kernel,
        in_specs=[hbm] * 3 + [vmem] * 3,
        out_specs=[vmem] * 2,
        out_shape=[jax.ShapeDtypeStruct((OWNED, E), F32), jax.ShapeDtypeStruct((256, E), F32)],
        scratch_shapes=[
            pltpu.VMEM(features.shape, BF16),
            pltpu.VMEM((STEPS, w_in.shape[0], STEP), BF16),
            pltpu.VMEM(upstream.shape, BF16),
            pltpu.VMEM((STEPS, SAMPLES, STEP), BF16),
            pltpu.VMEM((HOT_FIELDS, SAMPLES, E), BF16),
            pltpu.VMEM((HOT_FIELDS, SAMPLES, E), BF16),
            pltpu.VMEM((HOT_FIELDS, SAMPLES), I32),
            pltpu.VMEM((HOT_FIELDS * SAMPLES, 2 * E), BF16),
            pltpu.VMEM((2, 768, 2 * E), F32),
            pltpu.VMEM((4, 768, E), BF16),
            pltpu.VMEM((4, 768, E), BF16),
            pltpu.VMEM((8, 96, E), BF16),
            pltpu.VMEM((3, 32, E), F32),
            pltpu.VMEM((8, 96, E), BF16),
            pltpu.VMEM((3, 32, E), F32),
            pltpu.VMEM((12, 32, E), F32),
            pltpu.VMEM((8, 32, E), F32),
            pltpu.VMEM((3, LOOKUPS, E), BF16),
            pltpu.VMEM((3, 1, LOOKUPS), I32),
            pltpu.VMEM((LOOKUPS, E), F32),
            pltpu.VMEM((3, PLANE, SLOTS, E), BF16),
            pltpu.VMEM((3, PLANE, DEPTH, E), BF16),
            dma((STEPS + 2,)),
        ]
        + pairs(3) + pairs(3) + pairs(3, PLANE) + pairs(5) + pairs(4) + pairs(8) + pairs(12) + pairs(8),
        compiler_params=pltpu.CompilerParams(
            collective_id=0, has_side_effects=True, vmem_limit_bytes=56 << 20
        ),
        name="step",
    )(features, w_in, upstream, hot_ids, cold_rows, owners)


def adagrad(rows, accum, grads):
    accum_new = accum + jnp.mean(grads * grads, axis=1)
    return (rows - learn_rate * grads / jnp.sqrt(accum_new)[:, None], accum_new)


def shards(
    features,
    w_in,
    upstream,
    hot_ids,
    cold_rows,
    cold_owner,
    hot_table,
    hot_accum,
    cold_table,
    cold_accum,
):
    cold_sum, hot_sum = step(
        features, w_in, upstream, hot_ids.T, cold_rows.reshape(1, -1), cold_owner.reshape(1, -1)
    )
    hot_new, hot_accum_new = adagrad(hot_table, hot_accum, hot_sum)
    cold_new, cold_accum_new = adagrad(cold_table, cold_accum, cold_sum)
    return (hot_new, hot_accum_new, cold_new, cold_accum_new)


def solution(mesh):
    placed = (
        P(("grp", "shard"), None),
        P(),
        P(("grp", "shard"), None),
        P(("grp", "shard"), None),
        P(("grp", "shard")),
        P(("grp", "shard"), None),
        P("shard", None),
        P("shard"),
        P(("grp", "shard"), None),
        P(("grp", "shard")),
    )
    return jax.shard_map(
        shards,
        mesh=mesh,
        in_specs=placed,
        out_specs=(P("shard", None), P("shard"), P(("grp", "shard"), None), P(("grp", "shard"))),
        check_vma=False,
    )
```

time: 487 us -> 70.1 us (0.14)
  the two profiles are of different devices: /device:TPU:2 before, /device:TPU:4 now
where the time goes in v2:
time: 70.1 us; the launch traced here: 69.9 us
  Pallas kernels  62.9 us (90%)
  other arithmetic  6.21 us (9%)
  between operations  0.71 us (1%)
    pallas_call x1, Pallas kernels, step(): pl.pallas_call(step_kernel, in_specs=[hbm] * 3 + [vmem] * 3, out_specs=[v...  62.9 us
    sub x2, other arithmetic, adagrad(): return (rows - learn_rate * grads / jnp.sqrt(accum_new)[:, None], accum_new)  3.3 us
    reduce_sum x2, other arithmetic, adagrad(): accum_new = accum + jnp.mean(grads * grads, axis=1)  1.74 us

profile of v2, /device:TPU:4, one launch (start us, length us, event | category | flops | bytes accessed | tf_op | source)
XLA Modules:
  0.0 69.9 jit_solution(14761614963836044205)
XLA Ops:
  0.6 0.0 copy-start.3
  0.6 0.0 copy-start
  0.7 62.9 %step.1 = (f32[2048,128]{1,0:T(8,128)}, f32[256,128]{1,0:T(8,128)}) custom-call(bf16[256,1536]{1,0:T(8,128)(2,1)} %feat_hbm.1, bf16[1536,1024]{1,0:T(8,128)(2,1)} %w_hbm.1, bf16[256,1024]{1,0:T(8,128)(2,1)} %up_hbm.1, s32[8,256]{1,0:T(8,128)} %bitcast.3, s32[1,1024]{1,0:T(1,128)} %bitcast.4, s32[1,1024]{1,0:T(1,128)} %bitcast.5), custom_call_target="tpu_custom_call" | custom-call | tf_op jit(solution)/shard_map/step/pallas_call | solution.py:367
  63.6 0.0 copy-start.1
  63.6 0.0 copy-start.4
  63.6 0.0 copy-start.2
  63.6 1.6 %multiply_reduce_fusion = f32[2048]{0:T(1024)S(1)} fusion(f32[2048,128]{1,0:T(8,128)} %get-tuple-element.7), kind=kLoop, calls=%fused_computation.1 | loop fusion | flops 522240 | bytes 1056768 | tf_op jit(solution)/shard_map/reduce_sum | solution.py:406
  65.2 0.0 copy-done.3
  65.3 0.6 fusion
  65.9 0.0 copy-done
  65.9 2.5 %divide_subtract_fusion = f32[2048,128]{1,0:T(8,128)} fusion(f32[2048,128]{1,0:T(8,128)S(1)} %copy-done, f32[2048,128]{1,0:T(8,128)} %get-tuple-element.7, f32[2048]{0:T(1024)S(1)} %get-tuple-element.8), kind=kLoop, calls=%fused_computation | loop fusion | flops 786432 | bytes 3153920 | tf_op jit(solution)/shard_map/sub | solution.py:407
  68.4 0.0 copy-done.1
  68.4 0.1 multiply_reduce_fusion.1
  68.5 0.0 copy-done.4
  68.5 0.6 fusion.1
  69.1 0.0 copy-done.2
  69.1 0.8 %divide_subtract_fusion.1 = f32[256,128]{1,0:T(8,128)} fusion(f32[256,128]{1,0:T(8,128)S(1)} %copy-done.2, f32[256,128]{1,0:T(8,128)S(1)} %copy-done.1, f32[256]{0:T(256)S(1)} %get-tuple-element.10), kind=kLoop, calls=%fused_computation.2 | loop fusion | flops 98304 | bytes 394240 | tf_op jit(solution)/shard_map/sub | solution.py:407
Async XLA Ops:
  0.6 64.6 %copy-start.3 = (f32[2048]{0:T(1024)S(1)}, f32[2048]{0:T(1024)}, u32[]{:S(2)}) copy-start(f32[2048]{0:T(1024)} %param.19) | copy-start | bytes 24580
  0.6 65.2 %copy-start = (f32[2048,128]{1,0:T(8,128)S(1)}, f32[2048,128]{1,0:T(8,128)}, u32[]{:S(2)}) copy-start(f32[2048,128]{1,0:T(8,128)} %param.18) | copy-start | bytes 3145732
  63.6 4.8 %copy-start.1 = (f32[256,128]{1,0:T(8,128)S(1)}, f32[256,128]{1,0:T(8,128)}, u32[]{:S(2)}) copy-start(f32[256,128]{1,0:T(8,128)} %get-tuple-element.6) | copy-start | bytes 393220
  63.6 4.9 %copy-start.4 = (f32[256]{0:T(256)S(1)}, f32[256]{0:T(256)}, u32[]{:S(2)}) copy-start(f32[256]{0:T(256)} %param.17) | copy-start | bytes 3076
  63.6 5.5 %copy-start.2 = (f32[256,128]{1,0:T(8,128)S(1)}, f32[256,128]{1,0:T(8,128)}, u32[]{:S(2)}) copy-start(f32[256,128]{1,0:T(8,128)} %param.16) | copy-start | bytes 393220

commit v3 on v2

v3 whole, which is shorter than its diff:
```python
import jax
import jax.numpy as jnp
from jax import lax
from jax.experimental import pallas as pl
from jax.experimental.pallas import tpu as pltpu
from jax.sharding import PartitionSpec as P

MESH = pl.DeviceIdType.MESH
learn_rate = 0.5

E = 128
SAMPLES = 256
HOT_FIELDS, COLD_FIELDS = 8, 4
PLANE = 8
LOOKUPS = 1024
SLOTS = 96
USED = 85
HEAD = 88
DEPTH = 128
HALF = 512
OWNED = 2048
STEPS = 3
BLOCK = 512
PARTS = 4
BF16, F32, I32 = jnp.bfloat16, jnp.float32, jnp.int32


def iota(shape, axis):
    return lax.broadcasted_iota(I32, shape, axis)


def nt_dot(a, b):
    return lax.dot_general(a, b, (((1,), (1,)), ((), ())), preferred_element_type=F32)


def dot(a, b):
    return jnp.dot(a, b, preferred_element_type=F32)


def step_kernel(
    feat_hbm, w_hbm, up_hbm, ctab_hbm, htab_hbm, hid_hbm, row_hbm, own_hbm, cacc_hbm, hacc_hbm,
    hot_hbm, hot_accum_hbm, cold_hbm, cold_accum_hbm,
    feat, w, up, hid_ref, row_ref, own_ref, cacc_ref, hacc_ref, pre, delta, order, hotg, hotg2, hid2, wide, hacc, xsend, xrecv, ysend, yown, yrecv, zsend, zrecv, grecv,
    raw, packed, loose, parts, csend, crecv, csum, hsum, ctab, htab, cwas, hwas, cnow, hnow,
    l_s, r_ss, r_rs, p_ss, p_rs, c_ss, c_rs, h_ss, h_rs, x_ss, x_rs, y_ss, y_rs, z_ss, z_rs, g_ss, g_rs,
):
    g, s = lax.axis_index("grp"), lax.axis_index("shard")
    zl, y = g // 8, g % 8
    zh, x, c = s // 8, (s // 2) % 4, s % 2
    z = zh * 4 + zl

    def at(zh, x, c):
        return (zh * 4 + x) * 2 + c

    def plane_peer(k):
        return (g, at(zh, (x + k // 2) % 4, (c + k % 2) % 2))

    def y_peer(d):
        return (zl * 8 + (y + d) % 8, s)

    def z_peer(d):
        to = (z + d) % 12
        return ((to % 4) * 8 + y, at(to // 4, x, c))

    def copy(src, dst, ss, rs, peer):
        return pltpu.make_async_remote_copy(
            src_ref=src, dst_ref=dst, send_sem=ss, recv_sem=rs, device_id=peer, device_id_type=MESH
        )

    def raw_copy(q, h):
        rows = pl.ds(h * HALF, HALF)
        return copy(raw.at[0, rows], raw.at[q, rows], r_ss.at[q, h], r_rs.at[q, h], (g, at((zh + q) % 3, x, c)))

    def packed_copy(q):
        return copy(packed.at[0], packed.at[q], p_ss.at[q], p_rs.at[q], (g, at((zh + q) % 3, x, c)))

    def cold_copy(q, h, k):
        return copy(
            csend.at[q, h, k], crecv.at[q, h, k, pl.ds(0, SLOTS)], c_ss.at[q, h, k], c_rs.at[q, h, k], plane_peer(k)
        )

    def pair_copy(i):
        return copy(
            hotg.at[pl.ds(2 * i, 2)], hotg2.at[pl.ds(2 * i, 2)], h_ss.at[i], h_rs.at[i], plane_peer(1)
        )

    ids_copy = copy(hid_ref, hid2, h_ss.at[4], h_rs.at[4], plane_peer(1))

    def x_copy(d):
        return copy(xsend.at[d], xrecv.at[d], x_ss.at[d], x_rs.at[d], plane_peer(2 * d))

    def y_copy(d):
        return copy(ysend.at[d], yrecv.at[d], y_ss.at[d], y_rs.at[d], y_peer(d))

    def z_copy(d):
        return copy(zsend.at[((z + d) % 12) // 4], zrecv.at[z], z_ss.at[d], z_rs.at[d], z_peer(d))

    def g_copy(d):
        return copy(grecv.at[y], grecv.at[y], g_ss.at[d], g_rs.at[d], y_peer(d))

    def load(src, dst, i):
        return pltpu.make_async_copy(src, dst, l_s.at[i])

    def w_copy(j):
        rows = pl.ds(pl.multiple_of(j * BLOCK, BLOCK), BLOCK)
        return load(w_hbm.at[rows], w.at[rows], j)

    own_copy, row_copy = load(own_hbm, own_ref, STEPS), load(row_hbm, row_ref, STEPS + 1)
    feat_copy, up_copy, hid_copy = (
        load(feat_hbm, feat, STEPS + 2), load(up_hbm, up, STEPS + 3), load(hid_hbm, hid_ref, STEPS + 4)
    )
    late_copies = (
        load(cacc_hbm, cacc_ref, STEPS + 5),
        load(hacc_hbm, hacc_ref, STEPS + 6),
        load(ctab_hbm, ctab, STEPS + 7),
        load(htab_hbm, htab, STEPS + 8),
    )
    cold_out, cold_accum_out = load(ctab, cold_hbm, STEPS + 9), load(cnow, cold_accum_hbm, STEPS + 10)
    hot_out, hot_accum_out = load(htab, hot_hbm, STEPS + 11), load(hnow, hot_accum_hbm, STEPS + 12)
    own_copy.start()
    row_copy.start()
    feat_copy.start()
    for j in range(STEPS):
        w_copy(j).start()
    up_copy.start()
    hid_copy.start()
    for late in late_copies:
        late.start()

    barrier = pltpu.get_barrier_semaphore()

    def greet(peer):
        pl.semaphore_signal(barrier, inc=1, device_id=peer, device_id_type=MESH)

    for d in (4, 8, 1, 2, 3, 5, 6, 7, 9, 10, 11):
        greet(z_peer(d))
    for k in range(1, PLANE):
        greet(plane_peer(k))
    for d in range(1, 8):
        greet(y_peer(d))

    crecv[:, :, :, SLOTS:, :] = jnp.zeros((3, 2, PLANE, DEPTH - SLOTS, E), BF16)
    csum[...] = jnp.zeros_like(csum)
    hacc[...] = jnp.zeros_like(hacc)
    pre[...] = jnp.zeros_like(pre)

    own_copy.wait()
    row_copy.wait()
    owner = own_ref[...]
    named = (owner == iota((32, LOOKUPS), 0)).astype(F32)
    before = (iota((256, 256), 0) < iota((256, 256), 1)).astype(BF16)
    carry = jnp.zeros((32, 1), F32)
    ranks = []
    for b in range(LOOKUPS // 256):
        block = named[:, b * 256 : (b + 1) * 256]
        count = dot(block.astype(BF16), before) + carry
        ranks.append(jnp.sum(block * count, axis=0, keepdims=True))
        carry = carry + jnp.sum(block, axis=1, keepdims=True)
    rank = jnp.concatenate(ranks, axis=1).astype(I32)
    first = jnp.sum(jnp.where(iota((32, LOOKUPS), 0) < owner, carry, 0.0), axis=0, keepdims=True).astype(I32)
    spot = first + rank
    spot = spot % 2 * HALF + spot // 2
    for h in range(2):
        order[h] = (spot - h * HALF == iota((HALF, LOOKUPS), 0)).astype(BF16)
    digit = iota((8, LOOKUPS), 0)
    row = row_ref[...]
    digits = jnp.where(digit == 0, owner, jnp.where(digit == 1, rank // 2, jnp.where(digit == 2, row // 128, row % 128)))
    digits = jnp.where(digit < 4, digits, 0).astype(F32).astype(BF16)

    feat_copy.wait()

    def preact_step(j, carry):
        w_copy(j).wait()
        columns = pl.ds(pl.multiple_of(j * BLOCK, BLOCK), BLOCK)
        pre[...] += dot(feat[:, columns], w[columns, :])
        return carry

    lax.fori_loop(0, STEPS, preact_step, 0)
    up_copy.wait()
    preact = pre[...]
    sigm = jax.nn.sigmoid(preact)
    delta[...] = (up[...].astype(F32) * sigm * (1.0 + preact * (1.0 - sigm))).astype(BF16)
    total = nt_dot(delta[...], w[HOT_FIELDS * E :, :])
    for f in range(COLD_FIELDS):
        loose[pl.ds(f, SAMPLES, stride=COLD_FIELDS), :] = total[:, f * E : (f + 1) * E]
    cold_rows = loose[...].astype(BF16)

    pl.semaphore_wait(barrier, 11 + 7 + 7)
    for h in range(2):
        raw[0, h * HALF : (h + 1) * HALF, :] = dot(order[h], cold_rows).astype(BF16)
    for q in (1, 2):
        raw_copy(q, 0).start()
    hid_copy.wait()
    ids_copy.start()

    def hot_step(i, carry):
        rows = pl.ds(pl.multiple_of(i * 2 * E, 2 * E), 2 * E)
        total = nt_dot(delta[...], w[rows, :])
        hotg[2 * i] = total[:, :E].astype(BF16)
        hotg[2 * i + 1] = total[:, E:].astype(BF16)
        pair_copy(i).start()
        return carry

    lax.fori_loop(0, HOT_FIELDS // 2, hot_step, 0)

    for h in range(2):
        sent = nt_dot(digits, order[h]).astype(I32)
        packed[0, :, h * HALF : (h + 1) * HALF] = ((sent[0:1] * 128 + sent[1:2]) * 16 + sent[2:3]) * 128 + sent[3:4]
    for q in (1, 2):
        packed_copy(q).start()

    def hot_add(ids_ref, which, parity):
        ids = ids_ref[...]
        place = ids // 256
        away = ((place // 2) % 4 - x + 4) % 4
        inside = (place % 2 == c) & (away % 2 == parity)
        spot = jnp.where(inside, place // 8 * 256 + ids % 256, -1)
        for i in range(HOT_FIELDS // 2):
            chosen = jnp.concatenate(
                [(spot[2 * i + n : 2 * i + n + 1, :] == iota((768, SAMPLES), 0)).astype(BF16) for n in range(2)], axis=1
            )
            hacc[parity] += dot(chosen, wide[which, 2 * i * SAMPLES : (2 * i + 2) * SAMPLES, :])

    def widen(ids_ref, rows_ref, which):
        far = ((ids_ref[...] // 512) % 4 - x + 4) % 4 // 2
        far = far.astype(F32).T
        for f in range(HOT_FIELDS):
            keep = jnp.broadcast_to(far[:, f : f + 1], (SAMPLES, E)).astype(BF16)
            rows = rows_ref[f]
            second = rows * keep
            wide[which, f * SAMPLES : (f + 1) * SAMPLES, :E] = rows - second
            wide[which, f * SAMPLES : (f + 1) * SAMPLES, E:] = second

    widen(hid_ref, hotg, 0)
    hot_add(hid_ref, 0, 1)
    ids_copy.wait_recv()
    for i in range(HOT_FIELDS // 2):
        pair_copy(i).wait_recv()
    widen(hid2, hotg2, 1)
    hot_add(hid2, 1, 1)
    xsend[1] = hacc[1, :, :E].astype(BF16)
    x_copy(1).start()
    xsend[3] = hacc[1, :, E:].astype(BF16)
    x_copy(3).start()
    hot_add(hid_ref, 0, 0)
    hot_add(hid2, 1, 0)
    xsend[2] = hacc[0, :, E:].astype(BF16)
    x_copy(2).start()

    which = iota((8, E), 0)
    column = iota((8, E), 1)
    pick = jnp.where(
        (which == 0) & (column == 0) | (which == 1) & (column == 1), 1.0, 0.0
    ).astype(BF16)

    def number(q):
        row = packed[q] % OWNED
        sort = iota((E, LOOKUPS), 0)
        parts[q] = jnp.where(sort == 0, row // 128, jnp.where(sort == 1, row % 128, 0)).astype(F32).T.astype(BF16)

    def place(q, h):
        rows = pl.ds(h * HALF, HALF)
        held = jnp.concatenate([raw[q, rows, :], parts[q, rows, :]], axis=1)
        slot = packed[q, :, rows] // OWNED - at(zh, 0, 0) * DEPTH
        for b in range(2):
            chosen = (slot - b * 4 * DEPTH == iota((4 * DEPTH, HALF), 0)).astype(BF16)
            filled = dot(chosen, held)
            numbers = nt_dot(pick, filled[:, E:].astype(BF16))
            for n in range(4):
                to = b * 4 + n
                half = filled[n * DEPTH : n * DEPTH + SLOTS, :E]
                tail = half[HEAD:] + numbers[:, n * DEPTH : (n + 1) * DEPTH]
                k = (to // 2 - x + 4) % 4 * 2 + (to % 2 - c + 2) % 2
                csend[q, h, k] = jnp.concatenate([half[:HEAD], tail], axis=0).astype(BF16)

        def send(k, carry):
            cold_copy(q, h, k).start()
            return carry

        lax.fori_loop(1, PLANE, send, 0)
        crecv[q, h, 0, :SLOTS, :] = csend[q, h, 0]

    def cold_add(q, h, ks):
        ids, rows = [], []
        for k in ks:
            tile = crecv[q, h, k, SLOTS - 16 : SLOTS, :].astype(F32)
            row = jnp.where(iota((1, E), 1) < USED, tile[8:9] * 128.0 + tile[9:10], -1.0)
            far = jnp.broadcast_to((row >= OWNED // 2).astype(F32), (8, DEPTH)).T
            keep = jnp.broadcast_to(far[:, :1], (DEPTH, E)).astype(BF16)
            arrived = crecv[q, h, k]
            second = arrived * keep
            rows.append(jnp.concatenate([arrived - second, second], axis=1))
            ids.append(row.astype(I32))
        ids, rows = jnp.concatenate(ids, axis=1), jnp.concatenate(rows, axis=0)
        ids = jnp.where(ids < 0, -1, ids % (OWNED // 2))
        for b in range(OWNED // 512):
            chosen = (ids - b * 256 == iota((256, ids.shape[1]), 0)).astype(BF16)
            total = dot(chosen, rows)
            csum[b * 256 : (b + 1) * 256, :] += total[:, :E]
            csum[OWNED // 2 + b * 256 : OWNED // 2 + (b + 1) * 256, :] += total[:, E:]

    def cold_arrived(q, h):
        for k in range(1, 4):
            cold_copy(q, h, k).wait_recv()
        cold_add(q, h, range(4))
        for k in range(4, 8):
            cold_copy(q, h, k).wait_recv()
        cold_add(q, h, range(4, 8))

    def spread(was, accum_ref):
        def block(b, carry):
            rows = pl.ds(pl.multiple_of(b * E, E), E)
            was[rows, :] = jnp.broadcast_to(accum_ref[pl.ds(b, 1), :], (E, E)).T
            return carry

        lax.fori_loop(0, accum_ref.shape[0], block, 0)

    def adagrad(sum_ref, table, was, now_ref):
        ones = jnp.ones((2 * E, E), BF16)
        corner = iota((E, E), 0) == iota((E, E), 1)

        def block(b, carry):
            rows = pl.ds(pl.multiple_of(b * E, E), E)
            grads = sum_ref[rows, :]
            square = grads * grads
            high = square.astype(BF16)
            low = (square - high.astype(F32)).astype(BF16)
            now = was[rows, :] + dot(jnp.concatenate([high, low], axis=1), ones) * (1.0 / E)
            table[rows, :] = table[rows, :] - learn_rate * grads / jnp.sqrt(now)
            now_ref[pl.ds(b, 1), :] = jnp.sum(jnp.where(corner, now, 0.0), axis=0, keepdims=True)
            return carry

        lax.fori_loop(0, now_ref.shape[0], block, 0)

    number(0)
    place(0, 0)
    place(0, 1)
    for q in (1, 2):
        raw_copy(q, 0).wait_send()
        raw_copy(q, 1).start()
    for late in late_copies:
        late.wait()
    spread(cwas, cacc_ref)
    spread(hwas, hacc_ref)

    for d in (1, 3, 2):
        x_copy(d).wait_recv()

    def over_x(i, carry):
        rows = pl.ds(pl.multiple_of(i * 256, 256), 256)
        total = hacc[0, rows, :E]
        for d in range(1, 4):
            total = total + xrecv[d, rows, :].astype(F32)
        hacc[0, rows, :E] = total
        return carry

    lax.fori_loop(0, 3, over_x, 0)

    def to_y(d, carry):
        for i in range(3):
            rows = pl.ds(pl.multiple_of(((y + d) % 8) * 32 + i * 256, 32), 32)
            ysend[d, i * 32 : (i + 1) * 32, :] = hacc[0, rows, :E].astype(BF16)
        y_copy(d).start()
        return carry

    lax.fori_loop(1, 8, to_y, 0)
    for i in range(3):
        yown[i] = hacc[0, pl.ds(pl.multiple_of(y * 32 + i * 256, 32), 32), :E]

    cold_arrived(0, 0)
    cold_arrived(0, 1)
    for q in (1, 2):
        packed_copy(q).wait_recv()
        number(q)
    for q in (1, 2):
        raw_copy(q, 0).wait_recv()
        place(q, 0)

    for d in range(1, 8):
        y_copy(d).wait_recv()
    for i in range(3):
        total = yown[i]
        for d in range(1, 8):
            total = total + yrecv[d, i * 32 : (i + 1) * 32, :].astype(F32)
        zsend[i] = total.astype(BF16)
    zrecv[z] = zsend[zh]
    for d in range(1, 12):
        z_copy(d).start()

    cold_arrived(1, 0)
    cold_arrived(2, 0)
    for q in (1, 2):
        raw_copy(q, 1).wait_recv()
        place(q, 1)

    for d in range(1, 12):
        copy(zsend.at[zh], zrecv.at[(z + 12 - d) % 12], z_ss.at[d], z_rs.at[d], z_peer(d)).wait_recv()
    total = zrecv[0].astype(F32)
    for i in range(1, 12):
        total = total + zrecv[i].astype(F32)
    grecv[y] = total
    for d in range(1, 8):
        g_copy(d).start()

    cold_arrived(1, 1)
    cold_arrived(2, 1)
    adagrad(csum, ctab, cwas, cnow)
    cold_out.start()
    cold_accum_out.start()

    for d in range(1, 8):
        copy(grecv.at[y], grecv.at[(y + 8 - d) % 8], g_ss.at[d], g_rs.at[d], y_peer(d)).wait_recv()
    for i in range(8):
        hsum[i * 32 : (i + 1) * 32, :] = grecv[i]
    adagrad(hsum, htab, hwas, hnow)
    hot_out.start()
    hot_accum_out.start()

    for q in (1, 2):
        raw_copy(q, 1).wait_send()
        packed_copy(q).wait_send()
    ids_copy.wait_send()
    for i in range(HOT_FIELDS // 2):
        pair_copy(i).wait_send()

    def cold_sent(k, carry):
        for q in range(3):
            for h in range(2):
                cold_copy(q, h, k).wait_send()
        return carry

    lax.fori_loop(1, PLANE, cold_sent, 0)
    for d in range(1, 4):
        x_copy(d).wait_send()
    for d in range(1, 8):
        y_copy(d).wait_send()
        g_copy(d).wait_send()
    for d in range(1, 12):
        z_copy(d).wait_send()
    for out in (cold_out, cold_accum_out, hot_out, hot_accum_out):
        out.wait()


def hand_on_kernel(hot, hot_accum, cold, cold_accum, hot_out, hot_accum_out, cold_out, cold_accum_out, *held):
    sems = held[-1]
    rows = cold.shape[0] // PARTS
    ways = [(cold.at[pl.ds(i * rows, rows)], cold_out.at[pl.ds(i * rows, rows)]) for i in range(PARTS)]
    ways += [(hot, hot_out), (cold_accum, cold_accum_out), (hot_accum, hot_accum_out)]
    reads = [pltpu.make_async_copy(ways[i][0], held[i], sems.at[0, i]) for i in range(len(ways))]
    writes = [pltpu.make_async_copy(held[i], ways[i][1], sems.at[1, i]) for i in range(len(ways))]
    for read in reads:
        read.start()
    for read, write in zip(reads, writes):
        read.wait()
        write.start()
    for write in writes:
        write.wait()


def hand_on(*arrays):
    hbm = pl.BlockSpec(memory_space=pl.ANY)
    hot, hot_accum, cold, cold_accum = arrays
    held = [(cold.shape[0] // PARTS, E)] * PARTS + [hot.shape, cold_accum.shape, hot_accum.shape]
    return pl.pallas_call(
        hand_on_kernel,
        in_specs=[hbm] * 4,
        out_specs=[hbm] * 4,
        out_shape=[jax.ShapeDtypeStruct(each.shape, each.dtype) for each in arrays],
        scratch_shapes=[pltpu.VMEM(shape, F32) for shape in held] + [pltpu.SemaphoreType.DMA((2, len(held)))],
        compiler_params=pltpu.CompilerParams(vmem_limit_bytes=56 << 20),
        name="hand_on",
    )(*arrays)


def step(features, w_in, upstream, cold_table, hot_table, hot_ids, cold_rows, owners, cold_accum, hot_accum):
    hbm = pl.BlockSpec(memory_space=pl.ANY)
    dma = pltpu.SemaphoreType.DMA
    pairs = lambda *n: [dma(n), dma(n)]
    return pl.pallas_call(
        step_kernel,
        in_specs=[hbm] * 10,
        out_specs=[hbm] * 4,
        out_shape=[
            jax.ShapeDtypeStruct(each.shape, F32) for each in (hot_table, hot_accum, cold_table, cold_accum)
        ],
        scratch_shapes=[
            pltpu.VMEM(features.shape, BF16),
            pltpu.VMEM(w_in.shape, BF16),
            pltpu.VMEM(upstream.shape, BF16),
            pltpu.VMEM(hot_ids.shape, I32),
            pltpu.VMEM(cold_rows.shape, I32),
            pltpu.VMEM(owners.shape, I32),
            pltpu.VMEM(cold_accum.shape, F32),
            pltpu.VMEM(hot_accum.shape, F32),
            pltpu.VMEM(upstream.shape, F32),
            pltpu.VMEM(upstream.shape, BF16),
            pltpu.VMEM((2, HALF, LOOKUPS), BF16),
            pltpu.VMEM((HOT_FIELDS, SAMPLES, E), BF16),
            pltpu.VMEM((HOT_FIELDS, SAMPLES, E), BF16),
            pltpu.VMEM((HOT_FIELDS, SAMPLES), I32),
            pltpu.VMEM((2, HOT_FIELDS * SAMPLES, 2 * E), BF16),
            pltpu.VMEM((2, 768, 2 * E), F32),
            pltpu.VMEM((4, 768, E), BF16),
            pltpu.VMEM((4, 768, E), BF16),
            pltpu.VMEM((8, 96, E), BF16),
            pltpu.VMEM((3, 32, E), F32),
            pltpu.VMEM((8, 96, E), BF16),
            pltpu.VMEM((3, 32, E), BF16),
            pltpu.VMEM((12, 32, E), BF16),
            pltpu.VMEM((8, 32, E), F32),
            pltpu.VMEM((3, LOOKUPS, E), BF16),
            pltpu.VMEM((3, 1, LOOKUPS), I32),
            pltpu.VMEM((LOOKUPS, E), F32),
            pltpu.VMEM((3, LOOKUPS, E), BF16),
            pltpu.VMEM((3, 2, PLANE, SLOTS, E), BF16),
            pltpu.VMEM((3, 2, PLANE, DEPTH, E), BF16),
            pltpu.VMEM((OWNED, E), F32),
            pltpu.VMEM((256, E), F32),
            pltpu.VMEM((OWNED, E), F32),
            pltpu.VMEM((256, E), F32),
            pltpu.VMEM((OWNED, E), F32),
            pltpu.VMEM((256, E), F32),
            pltpu.VMEM((OWNED // E, E), F32),
            pltpu.VMEM((2, E), F32),
            dma((STEPS + 13,)),
        ]
        + pairs(3, 2) + pairs(3) + pairs(3, 2, PLANE) + pairs(5) + pairs(4) + pairs(8) + pairs(12) + pairs(8),
        compiler_params=pltpu.CompilerParams(
            collective_id=0, has_side_effects=True, vmem_limit_bytes=56 << 20
        ),
        name="step",
    )(features, w_in, upstream, cold_table, hot_table, hot_ids, cold_rows, owners, cold_accum, hot_accum)


def shards(
    features,
    w_in,
    upstream,
    hot_ids,
    cold_rows,
    cold_owner,
    hot_table,
    hot_accum,
    cold_table,
    cold_accum,
):
    results = step(
        features,
        w_in,
        upstream,
        cold_table,
        hot_table,
        hot_ids.T,
        cold_rows.reshape(1, -1),
        cold_owner.reshape(1, -1),
        cold_accum.reshape(-1, E),
        hot_accum.reshape(-1, E),
    )
    hot_new, hot_accum_new, cold_new, cold_accum_new = hand_on(*results)
    return (hot_new, hot_accum_new.reshape(-1), cold_new, cold_accum_new.reshape(-1))


def solution(mesh):
    placed = (
        P(("grp", "shard"), None),
        P(),
        P(("grp", "shard"), None),
        P(("grp", "shard"), None),
        P(("grp", "shard")),
        P(("grp", "shard"), None),
        P("shard", None),
        P("shard"),
        P(("grp", "shard"), None),
        P(("grp", "shard")),
    )
    return jax.shard_map(
        shards,
        mesh=mesh,
        in_specs=placed,
        out_specs=(P("shard", None), P("shard"), P(("grp", "shard"), None), P(("grp", "shard"))),
        check_vma=False,
    )
```

time: 70.1 us -> 65.5 us (0.934)
  the two profiles are of different devices: /device:TPU:4 before, /device:TPU:1 now
where the time goes in v3:
time: 65.5 us; the launch traced here: 65.3 us
  Pallas kernels  64.5 us (98%)
  between operations  0.8 us (1%)
    pallas_call x1, Pallas kernels, step(): pl.pallas_call(step_kernel, in_specs=[hbm] * 10, out_specs=[hbm] * 4, out...  62.5 us
    pallas_call x1, Pallas kernels, hand_on(): pl.pallas_call(hand_on_kernel, in_specs=[hbm] * 4, out_specs=[hbm] * 4, o...  2.08 us

profile of v3, /device:TPU:1, one launch (start us, length us, event | category | flops | bytes accessed | tf_op | source)
XLA Modules:
  0.0 65.3 jit_solution(6794749206488108376)
XLA Ops:
  0.6 62.5 %step.1 = (f32[256,128]{1,0:T(8,128)}, f32[2,128]{1,0:T(2,128)}, f32[2048,128]{1,0:T(8,128)}, f32[16,128]{1,0:T(8,128)}) custom-call(bf16[256,1536]{1,0:T(8,128)(2,1)} %feat_hbm.1, bf16[1536,1024]{1,0:T(8,128)(2,1)} %w_hbm.1, bf16[256,1024]{1,0:T(8,128)(2,1)} %up_hbm.1, f32[2048,128]{1,0:T(8,128)} %ctab_hbm.1, f32[256,128]{1,0:T(8,128)} %htab_hbm.1, ...), custom_call_target="tpu_custom_call" | custom-call | tf_op jit(solution)/shard_map/step/pallas_call | solution.py:479
  63.1 2.1 %hand_on.1 = (f32[256,128]{1,0:T(8,128)}, f32[2,128]{1,0:T(2,128)}, f32[2048,128]{1,0:T(8,128)}, f32[16,128]{1,0:T(8,128)}) custom-call(f32[256,128]{1,0:T(8,128)} %get-tuple-element.12.hot, f32[2,128]{1,0:T(2,128)} %get-tuple-element.13.hot_accum, f32[2048,128]{1,0:T(8,128)} %get-tuple-element.14.cold, f32[16,128]{1,0:T(8,128)} %get-tuple-element.15.cold_accum), custom_call_target="tpu_custom_call" | custom-call | tf_op jit(solution)/shard_map/hand_on/pallas_call | solution.py:464

commit v4 on v3

--- a/solution.py
+++ b/solution.py
@@ -203,12 +203,6 @@
 
     lax.fori_loop(0, HOT_FIELDS // 2, hot_step, 0)
 
-    for h in range(2):
-        sent = nt_dot(digits, order[h]).astype(I32)
-        packed[0, :, h * HALF : (h + 1) * HALF] = ((sent[0:1] * 128 + sent[1:2]) * 16 + sent[2:3]) * 128 + sent[3:4]
-    for q in (1, 2):
-        packed_copy(q).start()
-
     def hot_add(ids_ref, which, parity):
         ids = ids_ref[...]
         place = ids // 256
@@ -246,6 +240,12 @@
     hot_add(hid2, 1, 0)
     xsend[2] = hacc[0, :, E:].astype(BF16)
     x_copy(2).start()
+
+    for h in range(2):
+        sent = nt_dot(digits, order[h]).astype(I32)
+        packed[0, :, h * HALF : (h + 1) * HALF] = ((sent[0:1] * 128 + sent[1:2]) * 16 + sent[2:3]) * 128 + sent[3:4]
+    for q in (1, 2):
+        packed_copy(q).start()
 
     which = iota((8, E), 0)
     column = iota((8, E), 1)
@@ -315,19 +315,19 @@
 
         lax.fori_loop(0, accum_ref.shape[0], block, 0)
 
-    def adagrad(sum_ref, table, was, now_ref):
+    def adagrad(sum_ref, table, was, now_ref, tiles):
         ones = jnp.ones((2 * E, E), BF16)
-        corner = iota((E, E), 0) == iota((E, E), 1)
+        corner = iota((tiles, E, E), 1) == iota((tiles, E, E), 2)
 
         def block(b, carry):
-            rows = pl.ds(pl.multiple_of(b * E, E), E)
+            rows = pl.ds(pl.multiple_of(b * tiles * E, tiles * E), tiles * E)
             grads = sum_ref[rows, :]
             square = grads * grads
             high = square.astype(BF16)
             low = (square - high.astype(F32)).astype(BF16)
             now = was[rows, :] + dot(jnp.concatenate([high, low], axis=1), ones) * (1.0 / E)
             table[rows, :] = table[rows, :] - learn_rate * grads / jnp.sqrt(now)
-            now_ref[pl.ds(b, 1), :] = jnp.sum(jnp.where(corner, now, 0.0), axis=0, keepdims=True)
+            now_ref[b] = jnp.sum(jnp.where(corner, now.reshape(tiles, E, E), 0.0), axis=1)
             return carry
 
         lax.fori_loop(0, now_ref.shape[0], block, 0)
@@ -387,8 +387,6 @@
     for d in range(1, 12):
         z_copy(d).start()
 
-    cold_arrived(1, 0)
-    cold_arrived(2, 0)
     for q in (1, 2):
         raw_copy(q, 1).wait_recv()
         place(q, 1)
@@ -402,9 +400,10 @@
     for d in range(1, 8):
         g_copy(d).start()
 
-    cold_arrived(1, 1)
-    cold_arrived(2, 1)
-    adagrad(csum, ctab, cwas, cnow)
+    for h in range(2):
+        for q in (1, 2):
+            cold_arrived(q, h)
+    adagrad(csum, ctab, cwas, cnow, 8)
     cold_out.start()
     cold_accum_out.start()
 
@@ -412,7 +411,7 @@
         copy(grecv.at[y], grecv.at[(y + 8 - d) % 8], g_ss.at[d], g_rs.at[d], y_peer(d)).wait_recv()
     for i in range(8):
         hsum[i * 32 : (i + 1) * 32, :] = grecv[i]
-    adagrad(hsum, htab, hwas, hnow)
+    adagrad(hsum, htab, hwas, hnow, 2)
     hot_out.start()
     hot_accum_out.start()
 
@@ -481,7 +480,7 @@
         in_specs=[hbm] * 10,
         out_specs=[hbm] * 4,
         out_shape=[
-            jax.ShapeDtypeStruct(each.shape, F32) for each in (hot_table, hot_accum, cold_table, cold_accum)
+            jax.ShapeDtypeStruct(shape, F32) for shape in (hot_table.shape, (1, 2, E), cold_table.shape, (2, 8, E))
         ],
         scratch_shapes=[
             pltpu.VMEM(features.shape, BF16),
@@ -520,8 +519,8 @@
             pltpu.VMEM((256, E), F32),
             pltpu.VMEM((OWNED, E), F32),
             pltpu.VMEM((256, E), F32),
-            pltpu.VMEM((OWNED // E, E), F32),
-            pltpu.VMEM((2, E), F32),
+            pltpu.VMEM((2, 8, E), F32),
+            pltpu.VMEM((1, 2, E), F32),
             dma((STEPS + 13,)),
         ]
         + pairs(3, 2) + pairs(3) + pairs(3, 2, PLANE) + pairs(5) + pairs(4) + pairs(8) + pairs(12) + pairs(8),

time: 65.5 us -> 63.2 us (0.965)
  the two profiles are of different devices: /device:TPU:1 before, /device:TPU:4 now
where the time goes in v4:
time: 63.2 us; the launch traced here: 63.1 us
  Pallas kernels  62.2 us (98%)
  between operations  0.8 us (1%)
    pallas_call x1, Pallas kernels, step(): pl.pallas_call(step_kernel, in_specs=[hbm] * 10, out_specs=[hbm] * 4, out...  60.2 us
    pallas_call x1, Pallas kernels, hand_on(): pl.pallas_call(hand_on_kernel, in_specs=[hbm] * 4, out_specs=[hbm] * 4, o...  2.08 us

profile of v4, /device:TPU:4, one launch (start us, length us, event | category | flops | bytes accessed | tf_op | source)
XLA Modules:
  0.0 63.1 jit_solution(8555501329928232679)
XLA Ops:
  0.6 60.2 %step.1 = (f32[256,128]{1,0:T(8,128)}, f32[1,2,128]{2,1,0:T(2,128)}, f32[2048,128]{1,0:T(8,128)}, f32[2,8,128]{2,1,0:T(8,128)}) custom-call(bf16[256,1536]{1,0:T(8,128)(2,1)} %feat_hbm.1, bf16[1536,1024]{1,0:T(8,128)(2,1)} %w_hbm.1, bf16[256,1024]{1,0:T(8,128)(2,1)} %up_hbm.1, f32[2048,128]{1,0:T(8,128)} %ctab_hbm.1, f32[256,128]{1,0:T(8,128)} %htab_hbm.1, ...), custom_call_target="tpu_custom_call" | custom-call | tf_op jit(solution)/shard_map/step/pallas_call | solution.py:478
  60.8 2.1 %hand_on.1 = (f32[256,128]{1,0:T(8,128)}, f32[1,2,128]{2,1,0:T(2,128)}, f32[2048,128]{1,0:T(8,128)}, f32[2,8,128]{2,1,0:T(8,128)}) custom-call(f32[256,128]{1,0:T(8,128)} %get-tuple-element.12.hot, f32[1,2,128]{2,1,0:T(2,128)} %get-tuple-element.13.hot_accum, f32[2048,128]{1,0:T(8,128)} %get-tuple-element.14.cold, f32[2,8,128]{2,1,0:T(8,128)} %get-tuple-element.15.cold_accum), custom_call_target="tpu_custom_call" | custom-call | tf_op jit(solution)/shard_map/hand_on/pallas_call | solution.py:463

commit v5 on v4

--- a/solution.py
+++ b/solution.py
@@ -19,8 +19,8 @@
 DEPTH = 128
 HALF = 512
 OWNED = 2048
-STEPS = 3
-BLOCK = 512
+STEPS = 6
+BLOCK = 256
 PARTS = 4
 BF16, F32, I32 = jnp.bfloat16, jnp.float32, jnp.int32
 
@@ -368,7 +368,6 @@
         yown[i] = hacc[0, pl.ds(pl.multiple_of(y * 32 + i * 256, 32), 32), :E]
 
     cold_arrived(0, 0)
-    cold_arrived(0, 1)
     for q in (1, 2):
         packed_copy(q).wait_recv()
         number(q)
@@ -387,6 +386,7 @@
     for d in range(1, 12):
         z_copy(d).start()
 
+    cold_arrived(0, 1)
     for q in (1, 2):
         raw_copy(q, 1).wait_recv()
         place(q, 1)

time: 63.2 us -> 63.1 us (level)
  no operation moved by 1% of the time
where the time goes in v5:
time: 63.1 us; the launch traced here: 63 us
  Pallas kernels  62.2 us (99%)
  between operations  0.8 us (1%)
    pallas_call x1, Pallas kernels, step(): pl.pallas_call(step_kernel, in_specs=[hbm] * 10, out_specs=[hbm] * 4, out...  60.1 us
    pallas_call x1, Pallas kernels, hand_on(): pl.pallas_call(hand_on_kernel, in_specs=[hbm] * 4, out_specs=[hbm] * 4, o...  2.08 us

profile of v5, /device:TPU:4, one launch (start us, length us, event | category | flops | bytes accessed | tf_op | source)
XLA Modules:
  0.0 63.0 jit_solution(9720037489746170900)
XLA Ops:
  0.6 60.1 %step.1 = (f32[256,128]{1,0:T(8,128)}, f32[1,2,128]{2,1,0:T(2,128)}, f32[2048,128]{1,0:T(8,128)}, f32[2,8,128]{2,1,0:T(8,128)}) custom-call(bf16[256,1536]{1,0:T(8,128)(2,1)} %feat_hbm.1, bf16[1536,1024]{1,0:T(8,128)(2,1)} %w_hbm.1, bf16[256,1024]{1,0:T(8,128)(2,1)} %up_hbm.1, f32[2048,128]{1,0:T(8,128)} %ctab_hbm.1, f32[256,128]{1,0:T(8,128)} %htab_hbm.1, ...), custom_call_target="tpu_custom_call" | custom-call | tf_op jit(solution)/shard_map/step/pallas_call | solution.py:478
  60.7 2.1 %hand_on.1 = (f32[256,128]{1,0:T(8,128)}, f32[1,2,128]{2,1,0:T(2,128)}, f32[2048,128]{1,0:T(8,128)}, f32[2,8,128]{2,1,0:T(8,128)}) custom-call(f32[256,128]{1,0:T(8,128)} %get-tuple-element.12.hot, f32[1,2,128]{2,1,0:T(2,128)} %get-tuple-element.13.hot_accum, f32[2048,128]{1,0:T(8,128)} %get-tuple-element.14.cold, f32[2,8,128]{2,1,0:T(8,128)} %get-tuple-element.15.cold_accum), custom_call_target="tpu_custom_call" | custom-call | tf_op jit(solution)/shard_map/hand_on/pallas_call | solution.py:463
